TPU v7x, 512 devices: a whole 4x4x16 slice. The times are simulated.
512 devices in a mesh: lat: 64 (over x, z), chan: 8 (over y, core).
Axes of the slice: x: 4, y: 4, z: 16, core: 2. Of those that a mesh axis runs over, the one named last changes fastest.
Arguments:
- grid_field: bfloat16 [512, 1024, 384], P('lat', 'chan'), may hold values from -6 to 6
- norm_gain: float32 [384], replicated, may hold values from 0.25 to 1.75
- degree_gain: float32 [512, 384], replicated, may hold values from 0.25 to 4
- channel_mix: bfloat16 [2, 384, 384], replicated, may hold values from -0.21875 to 0.21875
Outputs:
- block_out: bfloat16 [512, 1024, 384], P('lat', None, 'chan')
All inputs are finite; a program needn't handle non-finite values.
Results may differ from a plain program's by a relative error of at most 0.02.
Values may be sent and summed in bfloat16 or wider, within the bound.
No kernel may reach another device: no remote copies, remote signals or barrier semaphores. Data moves between devices by JAX's collectives and lax.ppermute only.
A program may use at most 128 MiB of HBM per device.

v0:
```python
import math

import jax
import jax.numpy as jnp
from jax import lax
from jax.sharding import PartitionSpec as P

NLAT = 512
EMBED = 384
NLON = 1024
DEGREES = 512
MODES = 512


LGAMMA_HALF_THREE = 0.5 * math.log(math.pi) - math.log(2.0)


def grid_points():
    theta = math.pi * (jnp.arange(NLAT, dtype=jnp.float32) + 0.5) / NLAT
    cosines = jnp.cos(theta)
    harmonic = jnp.arange(1, NLAT // 2 + 1, dtype=jnp.float32)
    series = jnp.sum(
        jnp.cos(2.0 * harmonic[None, :] * theta[:, None]) / (4.0 * harmonic * harmonic - 1.0),
        axis=1,
    )
    weights = 2.0 / NLAT * (1.0 - 2.0 * series)
    return (cosines, weights)


def legendre(orders, cosines):
    order_col = orders[:, None]
    cos_row = cosines[None, :]
    log_sine = 0.5 * jnp.log(1.0 - cos_row * cos_row)
    log_start = (
        -0.5 * math.log(2.0)
        + 0.5 * (lax.lgamma(order_col + 1.5) - LGAMMA_HALF_THREE - lax.lgamma(order_col + 1.0))
        + order_col * log_sine
    )
    first_factor = jnp.sqrt(2.0 * order_col + 3.0)

    def advance(recur_state, degree):
        prev_one, prev_two, log_scale = recur_state
        level = degree.astype(jnp.float32)
        denom = jnp.maximum(level * level - order_col * order_col, 1.0)
        coef_a = jnp.sqrt(jnp.maximum(4.0 * level * level - 1.0, 1.0) / denom)
        coef_b = jnp.sqrt(
            jnp.maximum((level - 1.0) * (level - 1.0) - order_col * order_col, 0.0)
            * (2.0 * level + 1.0)
            / (denom * jnp.maximum(2.0 * level - 3.0, 1.0))
        )
        general = coef_a * cos_row * prev_one - coef_b * prev_two
        current = jnp.where(
            level == order_col,
            1.0,
            jnp.where(
                level == order_col + 1.0,
                first_factor * cos_row * prev_one,
                jnp.where(level > order_col + 1.0, general, 0.0),
            ),
        )
        log_scale = jnp.where(level == order_col, log_start, log_scale)
        values = current * jnp.exp(log_scale)
        oversize = jnp.abs(current) > 1000000000000.0
        factor = jnp.where(oversize, 2.0 ** (-40), 1.0)
        log_scale = log_scale + jnp.where(oversize, 40.0 * math.log(2.0), 0.0)
        return ((current * factor, prev_one * factor, log_scale), values)

    zeros = jnp.zeros((orders.shape[0], cosines.shape[0]), jnp.float32)
    final_state, values = lax.scan(
        advance, (zeros, zeros, zeros), jnp.arange(DEGREES, dtype=jnp.int32), unroll=16
    )
    return values


def pair_weight(channel_mix):
    real_part = channel_mix[0]
    imag_part = channel_mix[1]
    upper = jnp.concatenate([real_part, imag_part], axis=1)
    lower = jnp.concatenate([-imag_part, real_part], axis=1)
    return jnp.concatenate([upper, lower], axis=0)


def mode_order(owner_index, slot_index, lat_rows):
    return owner_index * lat_rows + slot_index


def split_product(form, data, table):
    table_high = table.astype(jnp.bfloat16)
    table_low = (table - table_high.astype(jnp.float32)).astype(jnp.bfloat16)
    first = jnp.einsum(form, data, table_high, preferred_element_type=jnp.float32)
    return first + jnp.einsum(form, data, table_low, preferred_element_type=jnp.float32)


def on_device(grid_field, norm_gain, degree_gain, channel_mix):
    lat_rows = grid_field.shape[0]
    lat_count = lax.axis_size("lat")
    chan_count = lax.axis_size("chan")
    chan_width = EMBED // chan_count
    values = grid_field.astype(jnp.float32)
    mean_value = jnp.mean(values, axis=2, keepdims=True)
    centered = values - mean_value
    variance = jnp.mean(centered * centered, axis=2, keepdims=True)
    normed = (centered * lax.rsqrt(variance + 1e-05) * norm_gain).astype(jnp.bfloat16)
    normed_cols, grid_cols = (
        lax.all_to_all(normed, "chan", split_axis=2, concat_axis=1, tiled=True),
        lax.all_to_all(grid_field, "chan", split_axis=2, concat_axis=1, tiled=True),
    )
    column = jnp.arange(2 * MODES, dtype=jnp.int32)
    col_orders = mode_order(column // (2 * lat_rows), column // 2 % lat_rows, lat_rows)
    col_parts = column % 2
    longitude = jnp.arange(NLON, dtype=jnp.int32)
    phase = longitude[:, None] * col_orders[None, :] % NLON
    angle = 2.0 * math.pi / NLON * phase.astype(jnp.float32)
    forward_dft = jnp.where(col_parts[None, :] == 0, jnp.cos(angle), -jnp.sin(angle)) / NLON
    spectrum = split_product("anc,nk->akc", normed_cols, forward_dft).astype(jnp.bfloat16)
    cosines, weights = grid_points()
    spectrum = spectrum.reshape(lat_rows, lat_count, 2 * lat_rows * chan_width)
    arrived = lax.all_to_all(spectrum, "lat", split_axis=1, concat_axis=0, tiled=True)
    modes_in = arrived.reshape(NLAT, lat_rows, 2, chan_width)
    own_orders = mode_order(
        lax.axis_index("lat"), jnp.arange(lat_rows, dtype=jnp.int32), lat_rows
    ).astype(jnp.float32)
    leg_values = legendre(own_orders, cosines)
    forward_table = (leg_values * weights).astype(jnp.bfloat16)
    inverse_table = leg_values.astype(jnp.bfloat16)
    own_gain = lax.dynamic_slice_in_dim(
        degree_gain, lax.axis_index("chan") * chan_width, chan_width, 1
    )
    all_coef = jnp.einsum(
        "ljn,njrc->ljrc", forward_table, modes_in, preferred_element_type=jnp.float32
    )
    coef_rows = (
        (all_coef * own_gain[:, None, None, :]).astype(jnp.bfloat16).reshape(-1, 2, chan_width)
    )
    row_count = coef_rows.shape[0]
    paired_weight = pair_weight(channel_mix)
    split_rows = coef_rows.reshape(chan_count, row_count // chan_count, 2, chan_width)
    piece = lax.all_to_all(split_rows, "chan", split_axis=0, concat_axis=3, tiled=True)
    count = piece.shape[1]
    flat_rows = piece.reshape(count, 2 * EMBED)
    mixed_flat = jnp.dot(flat_rows, paired_weight, preferred_element_type=jnp.float32).astype(
        jnp.bfloat16
    )
    mixed_rows = lax.all_to_all(
        mixed_flat.reshape(1, count, 2, EMBED), "chan", split_axis=3, concat_axis=0, tiled=True
    ).reshape(row_count, 2, chan_width)
    all_mixed = mixed_rows.reshape(DEGREES, lat_rows, 2, chan_width)
    field = jnp.einsum(
        "ljn,ljrc->njrc", inverse_table, all_mixed, preferred_element_type=jnp.float32
    ).astype(jnp.bfloat16)
    returned = lax.all_to_all(
        field.reshape(NLAT, 1, 2 * lat_rows * chan_width),
        "lat",
        split_axis=0,
        concat_axis=1,
        tiled=True,
    )
    returned = returned.reshape(lat_rows, 2 * MODES, chan_width)
    factor = jnp.where(col_orders == 0, 1.0, 2.0)
    inverse_dft = (
        jnp.where(col_parts[None, :] == 0, jnp.cos(angle), -jnp.sin(angle)) * factor[None, :]
    ).T
    restored = split_product("akc,kn->anc", returned, inverse_dft)
    return (grid_cols.astype(jnp.float32) + restored).astype(jnp.bfloat16)


def solution(mesh):
    return jax.shard_map(
        on_device,
        mesh=mesh,
        in_specs=(P("lat", "chan", None), P(), P(), P()),
        out_specs=P("lat", None, "chan"),
        check_vma=False,
    )
```

profile of v0, /device:TPU:6, one launch (start us, length us, event | category | flops | bytes accessed | tf_op | source)
XLA Modules:
  0.0 726.9 jit_solution(9631772766446253681)
XLA Ops:
  0.0 2.5 copy.52
  5.6 2.5 fusion.139
  8.1 4.5 all-to-all-start.1
  12.8 13.0 %all-to-all-done.1 = bf16[8,128,384]{1,0,2:T(8,128)(2,1)S(1)} async-done(((bf16[8,128,384]{1,0,2:T(8,128)(2,1)}), bf16[8,128,384]{1,0,2:T(8,128)(2,1)S(1)}, u32[]{:S(2)}, u32[]{:S(2)}) %all-to-all-start.1) | async-done | bytes 786464 | tf_op jit(solution)/shard_map/all_to_all | solution.py:105
  26.6 18.0 %fusion.133 = f32[1024,384]{0,1:S(1)} fusion(bf16[1024,384]{0,1:T(8,128)(2,1)S(1)} %bitcast.488, s32[1024]{0:T(1024)S(1)} %fusion.162, pred[1024]{0:T(1024)(128)(4,1)S(1)} %fusion.160), kind=kOutput, calls=%fused_computation.338 | convolution fusion | flops 824180736 | bytes 2364416
  44.6 18.2 %fusion.123 = f32[1024,384]{0,1:S(1)} fusion(bf16[1024,384]{0,1:T(8,128)(2,1)S(1)} %bitcast.489, s32[1024]{0:T(1024)S(1)} %fusion.162, pred[1024]{0:T(1024)(128)(4,1)S(1)} %fusion.160), kind=kOutput, calls=%fused_computation.331 | convolution fusion | flops 827326464 | bytes 2364416
  65.9 3.7 reshape.1586
  69.6 2.5 copy.59
  72.1 18.8 %all-to-all-start.2 = ((bf16[8,64,768]{2,0,1:T(8,128)(2,1)}), bf16[8,64,768]{2,0,1:T(8,128)(2,1)S(1)}, u32[]{:S(2)}, u32[]{:S(2)}) async-start(bf16[8,64,768]{2,0,1:T(8,128)(2,1)} %copy.59), calls=%async_computation.2 | async-start | bytes 1572864 | tf_op jit(solution)/shard_map/all_to_all | solution.py:118
  90.9 449.3 %while.23 = (s32[]{:T(128)}, f32[8,512]{1,0:T(8,128)S(1)}, f32[8,512]{1,0:T(8,128)S(1)}, f32[8,512]{1,0:T(8,128)S(1)}, f32[32,16,8,512]{3,2,1,0:T(8,128)}, /*ind...) while((s32[]{:T(128)}, f32[8,512]{1,0:T(8,128)S(1)}, ...), condition=%wide.region_3.4_spmd.clone.clone.clone.clone, body=%wide.region_2.3_spmd.clone.clone.clone.clone.sunk | while | flops 1670969 | bytes 2202716 | solution.py:69
  543.5 8.1 %reshape.1587 = bf16[512,8,2,48]{3,2,1,0:T(2,128)(2,1)S(1)} reshape(bf16[64,8,1,768]{3,1,0,2:T(8,128)(2,1)} %bitcast.480) | data formatting | bytes 1572864 | tf_op jit(solution)/shard_map/reshape | solution.py:119
  551.6 9.6 %fusion.141 = bf16[512,8,2,48]{0,3,2,1:T(8,128)(2,1)} fusion(f32[512,8,512]{2,1,0:T(8,128)} %bitcast.457, f32[512]{0:T(512)S(1)} %subtract_multiply_fusion, bf16[512,8,2,48]{3,2,1,0:T(2,128)(2,1)S(1)} %reshape.1587, f32[512,48]{0,1:T(8,128)S(1)} %copy.62), kind=kOutput, calls=%fused_computation.350 | convolution fusion | flops 407633920 | bytes 10061824 | tf_op jit(solution)/shard_map/ljn,njrc->ljrc/dot_general | solution.py:129
  561.2 2.7 copy.63
  565.6 3.5 all-to-all-start.3
  570.1 12.1 %all-to-all-done.3 = bf16[8,512,2,48]{1,3,2,0:T(8,128)(2,1)S(1)} async-done(((bf16[8,512,2,48]{1,3,2,0:T(8,128)(2,1)}), bf16[8,512,2,48]{1,3,2,0:T(8,128)(2,1)S(1)}, u32[]{:S(2)}, u32[]{:S(2)}) %all-to-all-start.3) | async-done | bytes 786464 | tf_op jit(solution)/shard_map/all_to_all | solution.py:138
  585.8 15.7 %all_to_all.87 = bf16[1,512,2,384]{1,2,0,3:T(2,128)(2,1)S(1)} all-to-all(bf16[1,512,2,384]{1,2,0,3:T(2,128)(2,1)S(1)} %copy.66), channel_id=1, replica_groups=mesh['lat'=64,'chan'=8] {'chan'}, dimensions={3} | all-to-all | bytes 1572864 | tf_op jit(solution)/shard_map/all_to_all | solution.py:144
  601.5 4.2 all-to-all-start
  608.7 9.4 %fusion.146 = bf16[8,2,48,512]{3,2,1,0:T(8,128)(2,1)} fusion(f32[512,8,512]{2,1,0:T(8,128)} %bitcast.458, bf16[512,8,2,48]{3,1,0,2:T(8,128)(2,1)S(1)} %bitcast.475), kind=kOutput, calls=%fused_computation.353 | convolution fusion | flops 403046400 | bytes 9961472 | tf_op jit(solution)/shard_map/ljn,ljrc->njrc/dot_general | solution.py:148
  618.5 2.3 reduce
  622.3 15.1 %all-to-all-start.5 = ((bf16[64,2,3072]{2,1,0:T(2,128)(2,1)}), bf16[64,2,3072]{2,1,0:T(2,128)(2,1)S(1)}, u32[]{:S(2)}, u32[]{:S(2)}) async-start(bf16[64,2,3072]{2,1,0:T(2,128)(2,1)} %reshape.1675), calls=%async_computation.5 | async-start | bytes 1572864 | tf_op jit(solution)/shard_map/all_to_all | solution.py:151
  639.6 41.2 %all-to-all-done.5 = bf16[64,2,3072]{2,1,0:T(2,128)(2,1)S(1)} async-done(((bf16[64,2,3072]{2,1,0:T(2,128)(2,1)}), bf16[64,2,3072]{2,1,0:T(2,128)(2,1)S(1)}, u32[]{:S(2)}, u32[]{:S(2)}) %all-to-all-start.5) | async-done | bytes 786464 | tf_op jit(solution)/shard_map/all_to_all | solution.py:151
  682.6 3.5 reshape.1595
  688.1 19.1 %fusion.129 = f32[1024,384]{0,1:S(1)} fusion(bf16[1024,384]{0,1:T(8,128)(2,1)} %bitcast.490, f32[1024]{0:T(1024)S(1)} %compare_select_fusion, s32[1024]{0:T(1024)S(1)} %fusion.162, pred[1024]{0:T(1024)(128)(4,1)S(1)} %fusion.160), kind=kOutput, calls=%fused_computation.336 | convolution fusion | flops 824180736 | bytes 2368512
  707.2 18.0 %fusion.124 = f32[1024,384]{0,1:S(1)} fusion(bf16[1024,384]{0,1:T(8,128)(2,1)S(1)} %bitcast.491, f32[1024]{0:T(1024)S(1)} %compare_select_fusion, s32[1024]{0:T(1024)S(1)} %fusion.162, pred[1024]{0:T(1024)(128)(4,1)S(1)} %fusion.160), kind=kOutput, calls=%fused_computation.332 | convolution fusion | flops 827326464 | bytes 2368512
  (2007 shorter events, 141.4 us)
Async XLA Ops:
  0.0 540.1 %copy-start = (f32[512,384]{1,0:T(8,128)S(1)}, f32[512,384]{1,0:T(8,128)}, u32[]{:S(2)}) copy-start(f32[512,384]{1,0:T(8,128)} %param.8) | copy-start | bytes 2359300
  8.1 17.6 %all-to-all-start.1 = ((bf16[8,128,384]{1,0,2:T(8,128)(2,1)}), bf16[8,128,384]{1,0,2:T(8,128)(2,1)S(1)}, u32[]{:S(2)}, u32[]{:S(2)}) async-start(bf16[8,128,384]{1,0,2:T(8,128)(2,1)} %fusion.139), calls=%async_computation.1 | async-start | bytes 1572864 | tf_op jit(solution)/shard_map/all_to_all | solution.py:105
  72.1 470.5 %all-to-all-start.2 = ((bf16[8,64,768]{2,0,1:T(8,128)(2,1)}), bf16[8,64,768]{2,0,1:T(8,128)(2,1)S(1)}, u32[]{:S(2)}, u32[]{:S(2)}) async-start(bf16[8,64,768]{2,0,1:T(8,128)(2,1)} %copy.59), calls=%async_computation.2 | async-start | bytes 1572864 | tf_op jit(solution)/shard_map/all_to_all | solution.py:118
  542.6 0.9 copy-start.2
  561.2 8.0 %copy-start.3 = (bf16[2,384,384]{2,1,0:T(8,128)(2,1)S(1)}, bf16[2,384,384]{2,1,0:T(8,128)(2,1)}, u32[]{:S(2)}) copy-start(bf16[2,384,384]{2,1,0:T(8,128)(2,1)} %param.9) | copy-start | bytes 1769476
  565.6 16.6 %all-to-all-start.3 = ((bf16[8,512,2,48]{1,3,2,0:T(8,128)(2,1)}), bf16[8,512,2,48]{1,3,2,0:T(8,128)(2,1)S(1)}, u32[]{:S(2)}, u32[]{:S(2)}) async-start(bf16[8,512,2,48]{1,3,2,0:T(8,128)(2,1)} %copy.64), calls=%async_computation.3 | async-start | bytes 1572864 | tf_op jit(solution)/shard_map/all_to_all | solution.py:138
  601.5 20.9 %all-to-all-start = ((bf16[8,128,384]{1,0,2:T(8,128)(2,1)}), bf16[8,128,384]{1,0,2:T(8,128)(2,1)}, u32[]{:S(2)}, u32[]{:S(2)}) async-start(bf16[8,128,384]{1,0,2:T(8,128)(2,1)} %copy.52), calls=%async_computation | async-start | bytes 1572864 | tf_op jit(solution)/shard_map/all_to_all | solution.py:106
  622.3 58.5 %all-to-all-start.5 = ((bf16[64,2,3072]{2,1,0:T(2,128)(2,1)}), bf16[64,2,3072]{2,1,0:T(2,128)(2,1)S(1)}, u32[]{:S(2)}, u32[]{:S(2)}) async-start(bf16[64,2,3072]{2,1,0:T(2,128)(2,1)} %reshape.1675), calls=%async_computation.5 | async-start | bytes 1572864 | tf_op jit(solution)/shard_map/all_to_all | solution.py:151
  688.1 19.1 %copy-start.4 = (bf16[8,1024,48]{1,2,0:T(8,128)(2,1)S(1)}, bf16[8,1024,48]{1,2,0:T(8,128)(2,1)}, u32[]{:S(2)}) copy-start(bf16[8,1024,48]{1,2,0:T(8,128)(2,1)} %copy.73) | copy-start | bytes 2359300
  707.2 18.0 %copy-start.1 = (bf16[8,128,384]{1,2,0:T(8,128)(2,1)S(1)}, bf16[8,128,384]{1,2,0:T(8,128)(2,1)}, u32[]{:S(2)}) copy-start(bf16[8,128,384]{1,2,0:T(8,128)(2,1)} %copy.53) | copy-start | bytes 2359300
where the time goes:
time: 741 us; the launch traced here: 727 us
  loops' own time  337 us (45%)
  matrix products  94.2 us (13%)
  local copies, waits for them, and re-layouts  88.5 us (12%)
  other arithmetic  78.7 us (11%)
  waiting for transfers between devices  66.3 us (9%)
  starting transfers between devices  46.2 us (6%)
  blocking collectives  15.7 us (2%)
    another operation x1, loops' own time, legendre(): lax.scan(advance, (zeros, zeros, zeros), jnp.arange(DEGREES, dtype=jnp.in...  337 us
    unnamed x4, matrix products  73.3 us
    while x480, other arithmetic  42.7 us
    all_to_all x1, waiting for transfers between devices, on_device(): lax.all_to_all(field.reshape(NLAT, 1, 2 * lat_rows * chan_width), 'lat',...  41.2 us
    dynamic_update_slice x32, local copies, waits for them, and re-layouts, legendre(): lax.scan(advance, (zeros, zeros, zeros), jnp.arange(DEGREES, dtype=jnp.in...  23.6 us
    slice x32, local copies, waits for them, and re-layouts, legendre(): lax.scan(advance, (zeros, zeros, zeros), jnp.arange(DEGREES, dtype=jnp.in...  23 us
    all_to_all x1, starting transfers between devices, on_device(): lax.all_to_all(spectrum, 'lat', split_axis=1, concat_axis=0, tiled=True)  18.8 us
    all_to_all x1, blocking collectives, on_device(): lax.all_to_all(mixed_flat.reshape(1, count, 2, EMBED), 'chan', split_axis...  15.7 us
  transfers between devices with their start and end apart: 5, of which 3 were waited for; matrix products, arithmetic and copies ran while one was open for 19% of the time, Pallas kernels for 0%

commit v1 on v0

v1 whole, which is shorter than its diff:
```python
import math

import jax
import jax.numpy as jnp
import numpy as np
from jax import lax
from jax.experimental import pallas as pl
from jax.experimental.pallas import tpu as pltpu
from jax.sharding import PartitionSpec as P

NLAT = 512
EMBED = 384
NLON = 1024
DEGREES = 512
MODES = 512
BLOCK = 8


def grid_points():
    theta = math.pi * (np.arange(NLAT, dtype=np.float64) + 0.5) / NLAT
    harmonic = np.arange(1, NLAT // 2 + 1, dtype=np.float64)
    series = np.sum(
        np.cos(2.0 * harmonic[None, :] * theta[:, None]) / (4.0 * harmonic * harmonic - 1.0),
        axis=1,
    )
    weights = 2.0 / NLAT * (1.0 - 2.0 * series)
    return theta, weights


def order_starts():
    return np.array(
        [
            0.5 * (math.lgamma(m + 1.5) - math.lgamma(1.5) - math.lgamma(m + 1.0) - math.log(2.0))
            / math.log(2.0)
            for m in range(MODES)
        ]
    )


def dft_tables():
    phase = np.arange(MODES)[:, None] * np.arange(NLON)[None, :] % NLON
    angle = 2.0 * math.pi / NLON * phase
    parts = np.stack([np.cos(angle), -np.sin(angle)], axis=1)
    factor = np.where(np.arange(MODES) == 0, 1.0, 2.0)[:, None, None]
    forward = (parts / NLON).reshape(2 * MODES, NLON)
    inverse = (parts * factor).reshape(2 * MODES, NLON)
    return forward.astype(jnp.bfloat16), inverse.astype(jnp.bfloat16)


def pair_weight(channel_mix):
    real_part = channel_mix[0]
    imag_part = channel_mix[1]
    upper = jnp.concatenate([real_part, imag_part], axis=1)
    lower = jnp.concatenate([-imag_part, real_part], axis=1)
    return jnp.concatenate([upper, lower], axis=0)


def legendre_kernel(coef_ref, rows_ref, forward_ref, inverse_ref):
    cos_row = rows_ref[0:1, :]
    start = rows_ref[1:2, :]
    exponent = rows_ref[2:3, :]
    weights = rows_ref[3:4, :]

    def block(index, state):
        one, two, power = state
        base = index * BLOCK
        rows = []
        for k in range(BLOCK):
            a = coef_ref[0, base + k]
            b = coef_ref[1, base + k]
            s = coef_ref[2, base + k]
            one, two = (a * cos_row) * one - b * two + s * start, one
            rows.append(one)
        values = jnp.concatenate(rows, axis=0) * jnp.exp2(power)
        here = pl.ds(pl.multiple_of(base, BLOCK), BLOCK)
        forward_ref[here, :] = values * weights
        inverse_ref[here, :] = values
        large = jnp.abs(one) > 1000.0
        factor = jnp.where(large, 2.0**-40, 1.0)
        power = power + jnp.where(large, 40.0, 0.0)
        return one * factor, two * factor, power

    zeros = jnp.zeros((1, NLAT), jnp.float32)
    lax.fori_loop(0, DEGREES // BLOCK, block, (zeros, zeros, exponent))


def legendre_tables(order):
    theta, weights = grid_points()
    cos_row = jnp.asarray(np.cos(theta), jnp.float32)
    log_sine = jnp.asarray(np.log2(np.sin(theta)), jnp.float32)
    starts = jnp.asarray(order_starts(), jnp.float32)
    start = lax.dynamic_slice_in_dim(starts, order, 1)[0]
    m = order.astype(jnp.float32)
    log_start = start + m * log_sine
    exponent = jnp.floor(log_start)
    mantissa = jnp.exp2(log_start - exponent)
    rows = jnp.stack([cos_row, mantissa, exponent, jnp.asarray(weights, jnp.float32)])
    level = jnp.arange(DEGREES, dtype=jnp.float32)
    denom = jnp.maximum(level * level - m * m, 1.0)
    above = level > m
    coef_a = jnp.where(above, jnp.sqrt(jnp.maximum(4.0 * level * level - 1.0, 1.0) / denom), 0.0)
    coef_b = jnp.sqrt(
        jnp.maximum((level - 1.0) * (level - 1.0) - m * m, 0.0)
        * (2.0 * level + 1.0)
        / (denom * jnp.maximum(2.0 * level - 3.0, 1.0))
    )
    coef_b = jnp.where(above, coef_b, 0.0)
    first = jnp.where(level == m, 1.0, 0.0)
    coefs = jnp.stack([coef_a, coef_b, first])
    shape = jax.ShapeDtypeStruct((DEGREES, NLAT), jnp.float32)
    return pl.pallas_call(
        legendre_kernel,
        out_shape=(shape, shape),
        in_specs=[
            pl.BlockSpec(memory_space=pltpu.SMEM),
            pl.BlockSpec(memory_space=pltpu.VMEM),
        ],
        out_specs=(
            pl.BlockSpec(memory_space=pltpu.VMEM),
            pl.BlockSpec(memory_space=pltpu.VMEM),
        ),
        cost_estimate=pl.CostEstimate(flops=40_000_000, bytes_accessed=2_000_000, transcendentals=32768),
        compiler_params=pltpu.CompilerParams(vmem_limit_bytes=16 * 1024 * 1024),
    )(coefs, rows)


def on_device(grid_field, norm_gain, degree_gain, channel_mix):
    both = ("lat", "chan")
    forward_dft, inverse_dft = dft_tables()
    own = lax.all_to_all(grid_field, "chan", split_axis=0, concat_axis=1, tiled=True)
    own = own.reshape(NLON, EMBED)
    values = own.astype(jnp.float32)
    mean_value = jnp.mean(values, axis=1, keepdims=True)
    centered = values - mean_value
    variance = jnp.mean(centered * centered, axis=1, keepdims=True)
    normed = (centered * lax.rsqrt(variance + 1e-05) * norm_gain).astype(jnp.bfloat16)
    spectrum = jnp.dot(forward_dft, normed, preferred_element_type=jnp.float32)
    spectrum = spectrum.astype(jnp.bfloat16).reshape(MODES, 2, EMBED)
    arrived = lax.all_to_all(spectrum, both, split_axis=0, concat_axis=0, tiled=True)
    forward_table, inverse_table = legendre_tables(lax.axis_index(both))
    forward_table = forward_table.astype(jnp.bfloat16)
    inverse_table = inverse_table.astype(jnp.bfloat16)
    coeffs = jnp.einsum("lj,jrc->lrc", forward_table, arrived, preferred_element_type=jnp.float32)
    scaled = (coeffs * degree_gain[:, None, :]).astype(jnp.bfloat16)
    mixed = jnp.dot(
        scaled.reshape(DEGREES, 2 * EMBED),
        pair_weight(channel_mix),
        preferred_element_type=jnp.float32,
    ).astype(jnp.bfloat16)
    field = jnp.einsum("lj,lk->jk", inverse_table, mixed, preferred_element_type=jnp.float32)
    field = field.astype(jnp.bfloat16).reshape(NLAT, 2, EMBED)
    returned = lax.all_to_all(field, both, split_axis=0, concat_axis=0, tiled=True)
    restored = jnp.einsum(
        "kn,kc->nc",
        inverse_dft,
        returned.reshape(2 * MODES, EMBED),
        preferred_element_type=jnp.float32,
    )
    block_out = (values + restored).astype(jnp.bfloat16)
    return lax.all_to_all(
        block_out.reshape(1, NLON, EMBED), "chan", split_axis=2, concat_axis=0, tiled=True
    )


def solution(mesh):
    return jax.shard_map(
        on_device,
        mesh=mesh,
        in_specs=(P("lat", "chan", None), P(), P(), P()),
        out_specs=P("lat", None, "chan"),
        check_vma=False,
    )
```

time: 741 us -> 183 us (0.25); the launches traced: 727 us -> 180 us
  loops' own time: 337 us -> 0 us
  matrix products: 94.2 us -> 10.1 us
  local copies, waits for them, and re-layouts: 88.5 us -> 10.5 us
  blocking collectives: 15.7 us -> 89.8 us
  other arithmetic: 78.7 us -> 7.71 us
  waiting for transfers between devices: 66.3 us -> 35.5 us
  starting transfers between devices: 46.2 us -> 23.1 us
    another operation x1 -> x0, loops' own time: 337 us -> none  [legendre(): lax.scan(advance, (zeros, zeros, zeros), jnp.arange(DEGREES, dtype=jnp.in...]
    all_to_all x1 -> x3, blocking collectives: 15.7 us -> 89.8 us  [the longest x1 56.3 us: on_device(): lax.all_to_all(field, both, split_axis=0, concat_axis=0, tiled=True)]
    unnamed x4 -> x0, matrix products: 73.3 us -> none
    while x480 -> x0, other arithmetic: 42.7 us -> none
    all_to_all x5 -> x1, waiting for transfers between devices: 66.3 us -> 35.5 us  [on_device(): lax.all_to_all(spectrum, both, split_axis=0, concat_axis=0, tiled=True)]
    dynamic_update_slice x32 -> x0, local copies, waits for them, and re-layouts: 23.6 us -> none  [legendre(): lax.scan(advance, (zeros, zeros, zeros), jnp.arange(DEGREES, dtype=jnp.in...]
    all_to_all x5 -> x1, starting transfers between devices: 46.2 us -> 23.1 us  [on_device(): lax.all_to_all(spectrum, both, split_axis=0, concat_axis=0, tiled=True)]
    slice x32 -> x0, local copies, waits for them, and re-layouts: 23 us -> none  [legendre(): lax.scan(advance, (zeros, zeros, zeros), jnp.arange(DEGREES, dtype=jnp.in...]
  transfers between devices with their start and end apart: 5 -> 1, of which waited for: 3 -> 1; matrix products, arithmetic and copies ran while one was open for 19% -> 3% of each run, Pallas kernels for 0% -> 2%
where the time goes in v1:
time: 183 us; the launch traced here: 180 us
  blocking collectives  89.8 us (49%)
  waiting for transfers between devices  35.5 us (19%)
  starting transfers between devices  23.1 us (13%)
  local copies, waits for them, and re-layouts  10.5 us (6%)
  matrix products  10.1 us (6%)
  other arithmetic  7.71 us (4%)
  Pallas kernels  3.06 us (2%)
    all_to_all x1, blocking collectives, on_device(): lax.all_to_all(field, both, split_axis=0, concat_axis=0, tiled=True)  56.3 us
    all_to_all x1, waiting for transfers between devices, on_device(): lax.all_to_all(spectrum, both, split_axis=0, concat_axis=0, tiled=True)  35.5 us
    all_to_all x1, starting transfers between devices, on_device(): lax.all_to_all(spectrum, both, split_axis=0, concat_axis=0, tiled=True)  23.1 us
    all_to_all x1, blocking collectives, on_device(): lax.all_to_all(grid_field, 'chan', split_axis=0, concat_axis=1, tiled=True)  17.8 us
    all_to_all x1, blocking collectives, on_device(): lax.all_to_all(block_out.reshape(1, NLON, EMBED), 'chan', split_axis=2, c...  15.7 us
    unnamed x1, other arithmetic  5.24 us
    unnamed x23, local copies, waits for them, and re-layouts  4.79 us
  transfers between devices with their start and end apart: 1, of which 1 were waited for; matrix products, arithmetic and copies ran while one was open for 3% of the time, Pallas kernels for 2%

profile of v1, /device:TPU:6, one launch (start us, length us, event | category | flops | bytes accessed | tf_op | source)
XLA Modules:
  0.0 179.8 jit_solution(17767599559530356446)
XLA Ops:
  0.0 17.8 %all_to_all.37 = bf16[8,128,384]{2,1,0:T(8,128)(2,1)S(1)} all-to-all(bf16[8,128,384]{2,1,0:T(8,128)(2,1)} %param.10), channel_id=1, replica_groups=mesh['lat'=64,'chan'=8] {'chan'}, dimensions={0} | all-to-all | bytes 1572864 | tf_op jit(solution)/shard_map/all_to_all | solution.py:130
  18.1 0.4 fusion.1
  18.9 0.5 copy-done.8
  19.4 1.0 fusion.7
  20.9 1.2 reshape.169
  22.0 23.1 %all-to-all-start.1 = ((bf16[512,2,384]{2,1,0:T(2,128)(2,1)}), bf16[512,2,384]{2,1,0:T(2,128)(2,1)}, u32[]{:S(2)}, u32[]{:S(2)}) async-start(bf16[512,2,384]{2,1,0:T(2,128)(2,1)} %reshape.169), calls=%async_computation.1 | async-start | bytes 1572864 | tf_op jit(solution)/shard_map/all_to_all | solution.py:139
  45.1 1.2 copy.20
  46.3 1.3 dynamic_slice.3
  47.7 0.6 multiply_exponential_fusion
  48.4 3.1 %shard_map.100 = (f32[512,512]{1,0:T(8,128)S(1)}, f32[512,512]{1,0:T(8,128)S(1)}) custom-call(f32[3,512]{1,0:T(4,128)S(1)} %pad_maximum_fusion.coef_ref, f32[4,512]{1,0:T(4,128)S(1)} %pad_maximum_fusion.1.rows_ref), custom_call_target="tpu_custom_call" | custom-call | flops 40000000 | bytes 2000000 | tf_op jit(solution)/shard_map/pallas_call | solution.py:111
  51.5 0.7 fusion.33
  52.2 0.9 slice_bitcast_fusion
  53.1 35.5 %all-to-all-done.1 = bf16[512,2,384]{2,1,0:T(2,128)(2,1)} async-done(((bf16[512,2,384]{2,1,0:T(2,128)(2,1)}), bf16[512,2,384]{2,1,0:T(2,128)(2,1)}, u32[]{:S(2)}, u32[]{:S(2)}) %all-to-all-start.1) | async-done | bytes 786464 | tf_op jit(solution)/shard_map/all_to_all | solution.py:139
  88.6 2.9 %multiply_convert_fusion = bf16[512,2,384]{0,2,1:T(8,128)(2,1)} fusion(bf16[512,2,384]{2,1,0:T(2,128)(2,1)} %all-to-all-done.1, f32[512,384]{0,1:T(8,128)} %copy.20, f32[512,512]{1,0:T(8,128)S(1)} %get-tuple-element.8), kind=kOutput, calls=%fused_computation.10 | convolution fusion | flops 403701760 | bytes 3407872 | tf_op jit(solution)/shard_map/lj,jrc->lrc/dot_general | solution.py:143
  91.5 3.2 %convolution_convert_fusion.1 = bf16[512,768]{1,0:T(8,128)(2,1)S(1)} fusion(bf16[512,768]{0,1:T(8,128)(2,1)} %bitcast.48, bf16[384,384]{1,0:T(8,128)(2,1)} %get-tuple-element.10, bf16[384,384]{1,0:T(8,128)(2,1)S(1)} %copy-done.2, bf16[384,384]{1,0:T(8,128)(2,1)S(1)} %copy-done.3, f32[512,512]{1,0:T(8,128)S(1)} %get-tuple-element.7), kind=kOutput, calls=%fused_computation.12 | convolution fusion | flops 1012400128 | bytes 3506176 | tf_op jit(solution)/shard_map/lj,lk->jk/dot_general | solution.py:150
  94.9 56.3 %all_to_all.38 = bf16[512,2,384]{2,1,0:T(2,128)(2,1)S(1)} all-to-all(bf16[512,2,384]{2,1,0:T(2,128)(2,1)S(1)} %reshape.171), channel_id=1, replica_groups=mesh['lat'=64,'chan'=8] {'lat','chan'}, dimensions={0} | all-to-all | bytes 1572864 | tf_op jit(solution)/shard_map/all_to_all | solution.py:152
  151.5 2.9 %fusion.6 = bf16[1,1024,384]{2,1,0:T(8,128)(2,1)S(1)} fusion(bf16[1024,1024]{1,0:T(8,128)(2,1)} %constant.56.clone, bf16[1024,384]{1,0:T(8,128)(2,1)S(1)} %reshape.172, bf16[8,128,384]{2,1,0:T(8,128)(2,1)S(1)} %all_to_all.37), kind=kOutput, calls=%fused_computation.14 | convolution fusion | flops 806486016 | bytes 4456448 | tf_op jit(solution)/shard_map/kn,kc->nc/dot_general | solution.py:153
  154.4 1.5 copy.21
  155.9 0.5 broadcast.204
  156.4 5.2 %reduce.8 = bf16[384,1024]{1,0:T(8,128)(2,1)S(1)} reduce(bf16[384,1,1024]{2,1,0:T(2,128)(2,1)S(1)} %bitcast.46, bf16[]{:T(256)} %broadcast.204), dimensions={1}, to_apply=%bitcast.39.reduce_sub_computation | reduce | bytes 1572866
  161.6 0.6 reshape.176
  162.2 15.7 %all_to_all.39 = bf16[8,2,24576]{2,1,0:T(2,128)(2,1)S(1)} all-to-all(bf16[8,2,24576]{2,1,0:T(2,128)(2,1)S(1)} %reshape.176), channel_id=1, replica_groups=mesh['lat'=64,'chan'=8] {'chan'}, dimensions={0} | all-to-all | bytes 1572864 | tf_op jit(solution)/shard_map/all_to_all | solution.py:160
  177.8 0.8 reshape.177
  178.7 1.2 copy.22
  (28 shorter events, 1.5 us)
Async XLA Ops:
  0.0 18.5 %copy-start.4 = (f32[384]{0:T(512)S(1)}, f32[384]{0:T(512)}, u32[]{:S(2)}) copy-start(f32[384]{0:T(512)} %param.11) | copy-start | bytes 4612
  17.8 1.6 copy-start.8
  20.8 24.3 %copy-start.1 = (f32[512,384]{1,0:T(8,128)S(1)}, f32[512,384]{1,0:T(8,128)}, u32[]{:S(2)}) copy-start(f32[512,384]{1,0:T(8,128)} %param.12) | copy-start | bytes 2359300
  22.0 25.7 %copy-start.5 = (f32[512]{0:T(512)S(1)}, f32[512]{0:T(512)}, u32[]{:S(2)}) copy-start(f32[512]{0:T(512)} %constant.53.clone) | copy-start | bytes 6148
  22.0 26.3 %copy-start.6 = (f32[1,512]{1,0:T(1,128)S(1)}, f32[1,512]{1,0:T(1,128)}, u32[]{:S(2)}) copy-start(f32[1,512]{1,0:T(1,128)} %constant.58) | copy-start | bytes 6148
  22.0 26.3 %copy-start.7 = (f32[1,512]{1,0:T(1,128)S(1)}, f32[1,512]{1,0:T(1,128)}, u32[]{:S(2)}) copy-start(f32[1,512]{1,0:T(1,128)} %constant.59) | copy-start | bytes 6148
  22.0 29.4 %copy-start = (bf16[2,384,384]{2,1,0:T(8,128)(2,1)S(1)}, bf16[2,384,384]{2,1,0:T(8,128)(2,1)}, u32[]{:S(2)}) copy-start(bf16[2,384,384]{2,1,0:T(8,128)(2,1)} %param.13) | copy-start | bytes 1769476
  22.0 66.5 %all-to-all-start.1 = ((bf16[512,2,384]{2,1,0:T(2,128)(2,1)}), bf16[512,2,384]{2,1,0:T(2,128)(2,1)}, u32[]{:S(2)}, u32[]{:S(2)}) async-start(bf16[512,2,384]{2,1,0:T(2,128)(2,1)} %reshape.169), calls=%async_computation.1 | async-start | bytes 1572864 | tf_op jit(solution)/shard_map/all_to_all | solution.py:139
  88.6 2.9 %copy-start.2 = (bf16[384,384]{1,0:T(8,128)(2,1)S(1)}, bf16[384,384]{1,0:T(8,128)(2,1)}, u32[]{:S(2)}) copy-start(bf16[384,384]{1,0:T(8,128)(2,1)} %fusion.33) | copy-start | bytes 884740
  88.6 2.9 %copy-start.3 = (bf16[384,384]{1,0:T(8,128)(2,1)S(1)}, bf16[384,384]{1,0:T(8,128)(2,1)}, u32[]{:S(2)}) copy-start(bf16[384,384]{1,0:T(8,128)(2,1)} %get-tuple-element.9) | copy-start | bytes 884740

commit v2 on v1

v2 whole, which is shorter than its diff:
```python
import math

import jax
import jax.numpy as jnp
import numpy as np
from jax import lax
from jax.experimental import pallas as pl
from jax.experimental.pallas import tpu as pltpu
from jax.sharding import PartitionSpec as P

NLAT = 512
EMBED = 384
NLON = 1024
DEGREES = 512
MODES = 512
VMEM_LIMIT = 16 * 1024 * 1024


def grid_points():
    theta = math.pi * (np.arange(NLAT, dtype=np.float64) + 0.5) / NLAT
    harmonic = np.arange(1, NLAT // 2 + 1, dtype=np.float64)
    series = np.sum(
        np.cos(2.0 * harmonic[None, :] * theta[:, None]) / (4.0 * harmonic * harmonic - 1.0),
        axis=1,
    )
    weights = 2.0 / NLAT * (1.0 - 2.0 * series)
    return theta, weights


def order_starts():
    return np.array(
        [
            0.5 * (math.lgamma(m + 1.5) - math.lgamma(1.5) - math.lgamma(m + 1.0) - math.log(2.0))
            / math.log(2.0)
            for m in range(MODES)
        ]
    )


def dft_tables():
    phase = np.arange(MODES)[:, None] * np.arange(NLON)[None, :] % NLON
    angle = 2.0 * math.pi / NLON * phase
    parts = np.stack([np.cos(angle), -np.sin(angle)], axis=1)
    factor = np.where(np.arange(MODES) == 0, 1.0, 2.0)[:, None, None]
    forward = (parts / NLON).transpose(1, 0, 2).reshape(2 * MODES, NLON)
    inverse = (parts * factor).reshape(2 * MODES, NLON)
    return forward.astype(jnp.bfloat16), inverse.astype(jnp.bfloat16)


def pair_weight(channel_mix):
    real_part = channel_mix[0]
    imag_part = channel_mix[1]
    upper = jnp.concatenate([real_part, imag_part], axis=1)
    lower = jnp.concatenate([-imag_part, real_part], axis=1)
    return jnp.concatenate([upper, lower], axis=0)


def permuted_latitudes():
    high, a, low = np.meshgrid(np.arange(4), np.arange(8), np.arange(16), indexing="ij")
    return ((16 * high + low) * 8 + a).reshape(-1)


def transform_kernel(grid_ref, gain_ref, table_ref, out_ref, normed_ref, held_ref, wide_ref, sem):
    copy = pltpu.make_async_copy(table_ref, held_ref, sem)
    copy.start()
    gain = gain_ref[...]
    for piece in range(8):
        rows = slice(128 * piece, 128 * piece + 128)
        values = grid_ref[rows, :].astype(jnp.float32)
        mean_value = jnp.mean(values, axis=1, keepdims=True)
        centered = values - mean_value
        variance = jnp.mean(centered * centered, axis=1, keepdims=True)
        normed_ref[rows, :] = (centered * lax.rsqrt(variance + 1e-05) * gain).astype(jnp.bfloat16)
    copy.wait()
    for r in range(2):
        spectrum = jnp.dot(
            held_ref[512 * r : 512 * r + 512, :],
            normed_ref[...],
            preferred_element_type=jnp.float32,
        )
        for t in range(3):
            wide_ref[pl.ds(2 * t + r, 512, stride=6), :] = spectrum[:, 128 * t : 128 * t + 128]
    out_ref[...] = wide_ref[...].astype(jnp.bfloat16)


def transform(grid, gain, table):
    vmem = pl.BlockSpec(memory_space=pltpu.VMEM)
    return pl.pallas_call(
        transform_kernel,
        out_shape=jax.ShapeDtypeStruct((6 * MODES, 128), jnp.bfloat16),
        in_specs=[vmem, vmem, pl.BlockSpec(memory_space=pl.ANY)],
        out_specs=vmem,
        scratch_shapes=[
            pltpu.VMEM((NLON, EMBED), jnp.bfloat16),
            pltpu.VMEM((2 * MODES, NLON), jnp.bfloat16),
            pltpu.VMEM((6 * MODES, 128), jnp.float32),
            pltpu.SemaphoreType.DMA,
        ],
        cost_estimate=pl.CostEstimate(
            flops=800_000_000, bytes_accessed=4_000_000, transcendentals=1024
        ),
        compiler_params=pltpu.CompilerParams(vmem_limit_bytes=VMEM_LIMIT),
    )(grid, gain, table)


def pack_rows(rows):
    return rows.reshape(512, 3, 2, 128).transpose(0, 2, 1, 3).reshape(512, 2, EMBED)


def unpack_rows(pieces):
    return pieces.reshape(512, 2, 3, 128).transpose(0, 2, 1, 3).reshape(3072, 128)


def legendre_kernel(
    coef_ref, cos_ref, start_ref, exponent_ref, weights_ref, table_ref, forward_ref, inverse_ref, held_ref
):
    held_ref[...] = table_ref[...]
    cos_rows = cos_ref[...]
    start = start_ref[...]
    weights = weights_ref[...]

    def block(index, state):
        one, two, power = state
        base = index * 16
        parts = []
        for half in range(2):
            rows = []
            for k in range(8):
                level = base + 8 * half + k
                a = coef_ref[0, level]
                b = coef_ref[1, level]
                s = coef_ref[2, level]
                one, two = (a * cos_rows) * one - b * two + s * start, one
                rows.append(one)
            scale = jnp.exp2(power)
            parts.append(
                [
                    jnp.concatenate([row[n : n + 1] for row in rows], axis=0) * scale[n : n + 1]
                    for n in range(2)
                ]
            )
            large = jnp.abs(one) > 1000.0
            factor = jnp.where(large, 2.0**-40, 1.0)
            power = power + jnp.where(large, 40.0, 0.0)
            one, two = one * factor, two * factor
        joined = [jnp.concatenate([parts[0][n], parts[1][n]], axis=0) for n in range(2)]
        here = pl.ds(pl.multiple_of(base, 16), 16)
        forward_ref[here, :] = (joined[0] * weights).astype(jnp.bfloat16)
        inverse_ref[here, :] = joined[1].astype(jnp.bfloat16)
        return one, two, power

    zeros = jnp.zeros((2, NLAT), jnp.float32)
    lax.fori_loop(0, DEGREES // 16, block, (zeros, zeros, exponent_ref[...]))


def legendre_tables(order, table):
    theta, weights = grid_points()
    theta_rows = np.stack([theta, theta[permuted_latitudes()]])
    cos_rows = jnp.asarray(np.cos(theta_rows), jnp.float32)
    log_sine = jnp.asarray(np.log2(np.sin(theta_rows)), jnp.float32)
    starts = jnp.asarray(order_starts(), jnp.float32)
    start = jnp.sum(jnp.where(jnp.arange(MODES) == order, starts, 0.0))
    m = order.astype(jnp.float32)
    log_start = start + m * log_sine
    exponent = jnp.floor(log_start)
    mantissa = jnp.exp2(log_start - exponent)
    level = jnp.arange(DEGREES, dtype=jnp.float32)
    denom = jnp.maximum(level * level - m * m, 1.0)
    above = level > m
    coef_a = jnp.where(above, jnp.sqrt(jnp.maximum(4.0 * level * level - 1.0, 1.0) / denom), 0.0)
    coef_b = jnp.sqrt(
        jnp.maximum((level - 1.0) * (level - 1.0) - m * m, 0.0)
        * (2.0 * level + 1.0)
        / (denom * jnp.maximum(2.0 * level - 3.0, 1.0))
    )
    coef_b = jnp.where(above, coef_b, 0.0)
    first = jnp.where(level == m, 1.0, 0.0)
    coefs = jnp.stack([coef_a, coef_b, first])
    vmem = pl.BlockSpec(memory_space=pltpu.VMEM)
    return pl.pallas_call(
        legendre_kernel,
        out_shape=(
            jax.ShapeDtypeStruct((DEGREES, NLAT), jnp.bfloat16),
            jax.ShapeDtypeStruct((DEGREES, NLAT), jnp.bfloat16),
            jax.ShapeDtypeStruct(table.shape, jnp.bfloat16),
        ),
        in_specs=[pl.BlockSpec(memory_space=pltpu.SMEM)] + [vmem] * 5,
        out_specs=(vmem, vmem, vmem),
        cost_estimate=pl.CostEstimate(
            flops=40_000_000, bytes_accessed=8_000_000, transcendentals=65536
        ),
        compiler_params=pltpu.CompilerParams(vmem_limit_bytes=VMEM_LIMIT),
    )(
        coefs,
        cos_rows,
        mantissa,
        exponent,
        jnp.asarray(weights, jnp.float32).reshape(1, NLAT),
        table,
    )


def mix_kernel(
    arrived_ref, forward_ref, gain_ref, weight_ref, inverse_ref, out_ref, wide_ref, field_ref
):
    wide_ref[...] = arrived_ref[...].astype(jnp.float32)
    gain = gain_ref[...]
    parts = []
    for r in range(2):
        spectrum = jnp.concatenate(
            [wide_ref[pl.ds(2 * t + r, 512, stride=6), :].astype(jnp.bfloat16) for t in range(3)],
            axis=1,
        )
        coeffs = jnp.dot(forward_ref[...], spectrum, preferred_element_type=jnp.float32)
        parts.append((coeffs * gain).astype(jnp.bfloat16))
    scaled = jnp.concatenate(parts, axis=1)
    mixed = lax.dot_general(
        weight_ref[...], scaled, (((1,), (1,)), ((), ())), preferred_element_type=jnp.float32
    ).astype(jnp.bfloat16)
    field_ref[...] = jnp.dot(mixed, inverse_ref[...], preferred_element_type=jnp.float32)
    lane = lax.broadcasted_iota(jnp.int32, (8, 128), 1)
    masks = {d: (lane & d) != 0 for d in (1, 2, 4, 8)}

    def group(index, carry):
        rows = pl.multiple_of(index // 4 * 16, 16)
        high = index % 4
        columns = pl.ds(pl.multiple_of(high * 128, 128), 128)
        halves = []
        for half in range(2):
            pieces = []
            for i in range(16):
                piece = field_ref[pl.ds(48 * i + rows + 8 * half, 8), columns]
                pieces.append(pltpu.roll(piece, i, 1) if i else piece)
            for d in (1, 2, 4, 8):
                pieces = [
                    jnp.where(masks[d], pieces[(k + d) % 16], pieces[k]) for k in range(16)
                ]
            halves.append(
                [pieces[0]] + [pltpu.roll(pieces[16 - low], 128 - low, 1) for low in range(1, 16)]
            )
        for low in range(16):
            both = jnp.concatenate([halves[0][low], halves[1][low]], axis=0)
            out_ref[high * 16 + low, pl.ds(rows, 16), :] = both.astype(jnp.bfloat16)
        return carry

    lax.fori_loop(0, 12, group, 0)


def mix_and_return(arrived, forward_table, gain, weight, inverse_table):
    vmem = pl.BlockSpec(memory_space=pltpu.VMEM)
    return pl.pallas_call(
        mix_kernel,
        out_shape=jax.ShapeDtypeStruct((64, 48, 128), jnp.bfloat16),
        in_specs=[vmem] * 5,
        out_specs=vmem,
        scratch_shapes=[
            pltpu.VMEM((6 * NLAT, 128), jnp.float32),
            pltpu.VMEM((2 * EMBED, NLAT), jnp.float32),
        ],
        cost_estimate=pl.CostEstimate(
            flops=1_400_000_000, bytes_accessed=4_000_000, transcendentals=0
        ),
        compiler_params=pltpu.CompilerParams(vmem_limit_bytes=VMEM_LIMIT),
    )(arrived, forward_table, gain, weight, inverse_table)


def restore_kernel(place_ref, spectrum_ref, table_ref, *refs):
    grid_refs, out_ref, field_ref = refs[:8], refs[8], refs[9]
    field_ref[...] = lax.dot_general(
        spectrum_ref[...],
        table_ref[...],
        (((0,), (0,)), ((), ())),
        preferred_element_type=jnp.float32,
    )
    for k in range(8):
        columns = pl.ds(pl.multiple_of(place_ref[k] * 128, 128), 128)
        for a in range(8):
            for t in range(3):
                piece = field_ref[(8 * t + a) * 16 : (8 * t + a) * 16 + 16, columns]
                rows = slice(16 * t, 16 * t + 16)
                own = grid_refs[k][a, rows, :].astype(jnp.float32)
                out_ref[a, rows, columns] = (own + piece).astype(jnp.bfloat16)


def restore(spectrum, table, grids, places):
    vmem = pl.BlockSpec(memory_space=pltpu.VMEM)
    return pl.pallas_call(
        restore_kernel,
        out_shape=jax.ShapeDtypeStruct((8, 48, NLON), jnp.bfloat16),
        in_specs=[pl.BlockSpec(memory_space=pltpu.SMEM)] + [vmem] * 10,
        out_specs=vmem,
        scratch_shapes=[pltpu.VMEM((EMBED, NLON), jnp.float32)],
        cost_estimate=pl.CostEstimate(
            flops=800_000_000, bytes_accessed=4_000_000, transcendentals=0
        ),
        compiler_params=pltpu.CompilerParams(vmem_limit_bytes=VMEM_LIMIT),
    )(places, spectrum, table, *grids)


def mix_weight(channel_mix):
    paired = pair_weight(channel_mix).T.reshape(2, 24, 16, 2 * EMBED)
    return paired.transpose(2, 1, 0, 3).reshape(2 * EMBED, 2 * EMBED)


def on_device(grid_field, norm_gain, degree_gain, channel_mix):
    both = ("lat", "chan")
    place = lax.axis_index("chan")
    forward_dft, inverse_dft = dft_tables()
    own = lax.all_to_all(grid_field, "chan", split_axis=0, concat_axis=0, tiled=True)
    own = own.reshape(NLON, EMBED)
    spectrum = pack_rows(transform(own, norm_gain.reshape(1, EMBED), jnp.asarray(forward_dft)))
    spectrum, grid_later, channel_mix = lax.optimization_barrier(
        (spectrum, grid_field, channel_mix)
    )
    arrived = lax.all_to_all(spectrum, both, split_axis=0, concat_axis=0, tiled=True)
    forward_table, inverse_table, table = legendre_tables(
        lax.axis_index(both), jnp.asarray(inverse_dft)
    )
    weight = mix_weight(channel_mix)
    pieces = grid_later.transpose(0, 2, 1).reshape(8, 8, 48, 128).transpose(1, 0, 2, 3)
    grids = [lax.dynamic_index_in_dim(pieces, place ^ k, 0, keepdims=False) for k in range(8)]
    grids = [grids[0]] + [
        lax.ppermute(grids[k], "chan", [(i, i ^ k) for i in range(8)]) for k in range(1, 8)
    ]
    places = jnp.arange(8, dtype=jnp.int32) ^ place
    arrived, forward_table, inverse_table, weight = lax.optimization_barrier(
        (arrived, forward_table, inverse_table, weight)
    )
    field = mix_and_return(unpack_rows(arrived), forward_table, degree_gain, weight, inverse_table)
    returned = lax.all_to_all(
        pack_rows(field.reshape(3072, 128)), both, split_axis=0, concat_axis=0, tiled=True
    )
    block_out = restore(returned.reshape(2 * MODES, EMBED), table, grids, places)
    return block_out.transpose(0, 2, 1)


def solution(mesh):
    return jax.shard_map(
        on_device,
        mesh=mesh,
        in_specs=(P("lat", "chan", None), P(), P(), P()),
        out_specs=P("lat", None, "chan"),
        check_vma=False,
    )
```

time: 183 us -> 160 us (0.87)
  blocking collectives: 89.8 us -> 0 us
  starting transfers between devices: 23.1 us -> 62.1 us
  waiting for transfers between devices: 35.5 us -> 61.2 us
  Pallas kernels: 3.06 us -> 15.6 us
  matrix products: 10.1 us -> 0 us
  other arithmetic: 7.71 us -> 1.55 us
  local copies, waits for them, and re-layouts: 10.5 us -> 16.5 us
    all_to_all x3 -> x0, blocking collectives: 89.8 us -> none  [the longest x1 56.3 us: on_device(): lax.all_to_all(field, both, split_axis=0, concat_axis=0, tiled=True)]
    all_to_all x0 -> x2, waiting for transfers between devices: none -> 31.3 us  [the longest x1 18.8 us: on_device(): lax.all_to_all(pack_rows(field.reshape(3072, 128)), both, split_axis=0, c...]
    ppermute x0 -> x7, starting transfers between devices: none -> 21.4 us  [on_device(): lax.ppermute(grids[k], 'chan', [(i, i ^ k) for i in range(8)])]
    all_to_all x0 -> x2, starting transfers between devices: none -> 17.6 us  [the longest x1 13.2 us: on_device(): lax.all_to_all(pack_rows(field.reshape(3072, 128)), both, split_axis=0, c...]
    pallas_call x1 -> x4, Pallas kernels: 3.06 us -> 15.6 us  [the longest x1 6.38 us: mix_and_return(): pl.pallas_call(mix_kernel, out_shape=jax.ShapeDtypeStruct((64, 48, 128),...]
    dot_general x4 -> x0, matrix products: 10.1 us -> none  [the longest x1 3.21 us: on_device(): jnp.einsum('lj,lk->jk', inverse_table, mixed, preferred_element_type=jnp....]
    all_to_all x1, waiting for transfers between devices: 35.5 us -> 29.9 us  [on_device(): lax.all_to_all(spectrum, both, split_axis=0, concat_axis=0, tiled=True)]
    unnamed x1 -> x0, other arithmetic: 5.24 us -> none
  transfers between devices with their start and end apart: 1 -> 10, of which waited for: 1 -> 3; matrix products, arithmetic and copies ran while one was open for 3% -> 9% of each run, Pallas kernels for 2% -> 2%
where the time goes in v2:
time: 160 us; the launch traced here: 157 us
  starting transfers between devices  62.1 us (39%)
  waiting for transfers between devices  61.2 us (38%)
  local copies, waits for them, and re-layouts  16.5 us (10%)
  Pallas kernels  15.6 us (10%)
    all_to_all x1, waiting for transfers between devices, on_device(): lax.all_to_all(spectrum, both, split_axis=0, concat_axis=0, tiled=True)  29.9 us
    all_to_all x1, starting transfers between devices, on_device(): lax.all_to_all(spectrum, both, split_axis=0, concat_axis=0, tiled=True)  23.1 us
    ppermute x7, starting transfers between devices, on_device(): lax.ppermute(grids[k], 'chan', [(i, i ^ k) for i in range(8)])  21.4 us
    all_to_all x1, waiting for transfers between devices, on_device(): lax.all_to_all(pack_rows(field.reshape(3072, 128)), both, split_axis=0, c...  18.8 us
    all_to_all x1, starting transfers between devices, on_device(): lax.all_to_all(pack_rows(field.reshape(3072, 128)), both, split_axis=0, c...  13.2 us
    all_to_all x1, waiting for transfers between devices, on_device(): lax.all_to_all(grid_field, 'chan', split_axis=0, concat_axis=0, tiled=True)  12.5 us
    pallas_call x1, Pallas kernels, mix_and_return(): pl.pallas_call(mix_kernel, out_shape=jax.ShapeDtypeStruct((64, 48, 128),...  6.38 us
    all_to_all x1, starting transfers between devices, on_device(): lax.all_to_all(grid_field, 'chan', split_axis=0, concat_axis=0, tiled=True)  4.47 us
  transfers between devices with their start and end apart: 10, of which 3 were waited for; matrix products, arithmetic and copies ran while one was open for 9% of the time, Pallas kernels for 2%

profile of v2, /device:TPU:6, one launch (start us, length us, event | category | flops | bytes accessed | tf_op | source)
XLA Modules:
  0.0 157.3 jit_solution(13921179013867961670)
XLA Ops:
  0.0 4.5 %all-to-all-start = ((bf16[8,128,384]{2,1,0:T(8,128)(2,1)}), bf16[8,128,384]{2,1,0:T(8,128)(2,1)S(1)}, u32[]{:S(2)}, u32[]{:S(2)}) async-start(bf16[8,128,384]{2,1,0:T(8,128)(2,1)} %param.10), calls=%async_computation | async-start | bytes 1572864 | tf_op jit(solution)/shard_map/all_to_all | solution.py:309
  5.2 12.5 %all-to-all-done = bf16[8,128,384]{2,1,0:T(8,128)(2,1)S(1)} async-done(((bf16[8,128,384]{2,1,0:T(8,128)(2,1)}), bf16[8,128,384]{2,1,0:T(8,128)(2,1)S(1)}, u32[]{:S(2)}, u32[]{:S(2)}) %all-to-all-start) | async-done | bytes 786464 | tf_op jit(solution)/shard_map/all_to_all | solution.py:309
  17.6 1.6 %copy-done.3 = bf16[1024,1024]{1,0:T(8,128)(2,1)S(1)} copy-done((bf16[1024,1024]{1,0:T(8,128)(2,1)S(1)}, bf16[1024,1024]{1,0:T(8,128)(2,1)}, u32[]{:S(2)}) %copy-start.3) | copy-done | bytes 2097176
  19.2 3.0 %shard_map.100 = bf16[3072,128]{1,0:T(8,128)(2,1)} custom-call(bf16[1024,384]{1,0:T(8,128)(2,1)S(1)} %bitcast.47, f32[1,384]{1,0:T(1,128)S(1)} %reshape.155.gain_ref, bf16[1024,1024]{1,0:T(8,128)(2,1)S(1)} %copy-done.3), custom_call_target="tpu_custom_call" | custom-call | flops 800000000 | bytes 4000000 | tf_op jit(solution)/shard_map/pallas_call | solution.py:88
  22.2 23.1 %all-to-all-start.1 = ((bf16[512,2,384]{2,1,0:T(2,128)(2,1)}), bf16[512,2,384]{2,1,0:T(2,128)(2,1)}, u32[]{:S(2)}, u32[]{:S(2)}) async-start(bf16[512,2,384]{2,1,0:T(2,128)(2,1)} %bitcast.3), calls=%async_computation.1 | async-start | bytes 1572864 | tf_op jit(solution)/shard_map/all_to_all | solution.py:315
  46.8 3.1 %shard_map.101 = (bf16[512,512]{1,0:T(8,128)(2,1)S(1)}, bf16[512,512]{1,0:T(8,128)(2,1)S(1)}, bf16[1024,1024]{1,0:T(8,128)(2,1)S(1)}) custom-call(f32[3,512]{1,0:T(4,128)S(1)} %pad_maximum_fusion.coef_ref, f32[2,512]{1,0:T(2,128)S(1)} %copy-done.4, f32[2,512]{1,0:T(2,128)S(1)} %get-tuple-element.36.start_ref, f32[2,512]{1,0:T(2,128)S(1)} %get-tuple-element.35.exponent_ref, ...), custom_call_target="tpu_custom_call" | custom-call | flops 40000000 | bytes 8000000 | tf_op jit(solution)/shard_map/pallas_call | solution.py:180
  50.0 1.3 copy-done.1
  52.1 1.4 copy.20
  53.7 2.2 %copy.22 = bf16[16,24,2,768]{3,2,1,0:T(2,128)(2,1)} copy(bf16[16,24,2,768]{3,0,1,2:T(8,128)(2,1)S(1)} %bitcast.48) | data formatting | bytes 2359296 | tf_op jit(solution)/shard_map/transpose | solution.py:302
  55.9 3.0 %reshape.160.weight_ref = bf16[768,768]{1,0:T(8,128)(2,1)S(1)} reshape(bf16[16,24,2,768]{3,2,1,0:T(2,128)(2,1)} %copy.22) | data formatting | bytes 2359296 | tf_op jit(solution)/shard_map/reshape | solution.py:302
  58.9 29.9 %all-to-all-done.1 = bf16[512,2,384]{2,1,0:T(2,128)(2,1)} async-done(((bf16[512,2,384]{2,1,0:T(2,128)(2,1)}), bf16[512,2,384]{2,1,0:T(2,128)(2,1)}, u32[]{:S(2)}, u32[]{:S(2)}) %all-to-all-start.1) | async-done | bytes 786464 | tf_op jit(solution)/shard_map/all_to_all | solution.py:315
  88.8 6.4 %shard_map.102 = bf16[64,48,128]{2,1,0:T(8,128)(2,1)} custom-call(bf16[3072,128]{1,0:T(8,128)(2,1)} %bitcast.11.arrived_ref, bf16[512,512]{1,0:T(8,128)(2,1)S(1)} %get-tuple-element.20.forward_ref, f32[512,384]{1,0:T(8,128)S(1)} %copy-done.6, bf16[768,768]{1,0:T(8,128)(2,1)S(1)} %reshape.160.weight_ref, bf16[512,512]{1,0:T(8,128)(2,1)S(1)} %copy-done.8), custom_call_target="tpu_custom_call" | custom-call | flops 1400000000 | bytes 4000000 | tf_op jit(solution)/shard_map/pallas_call | solution.py:251
  95.2 13.2 %all-to-all-start.2 = ((bf16[512,2,384]{2,1,0:T(2,128)(2,1)}), bf16[512,2,384]{2,1,0:T(2,128)(2,1)}, u32[]{:S(2)}, u32[]{:S(2)}) async-start(bf16[512,2,384]{2,1,0:T(2,128)(2,1)} %bitcast.14), calls=%async_computation.2 | async-start | bytes 1572864 | tf_op jit(solution)/shard_map/all_to_all | solution.py:330
  109.6 2.0 %dynamic-slice_bitcast_fusion = (bf16[8,48,128]{2,1,0:T(8,128)(2,1)}, bf16[8,48,128]{2,1,0:T(8,128)(2,1)}, bf16[8,48,128]{2,1,0:T(8,128)(2,1)}, bf16[8,48,128]{2...) fusion(bf16[8,8,48,128]{3,2,1,0:T(8,128)(2,1)} %bitcast.49, ...), kind=kLoop, calls=%fused_computation.3 | loop fusion | bytes 1572896 | tf_op jit(solution)/shard_map/jit(dynamic_index_in_dim)/squeeze | solution.py:321
  111.6 2.0 %collective-permute-start = (bf16[8,48,128]{2,1,0:T(8,128)(2,1)S(1)}, bf16[8,48,128]{2,1,0:T(8,128)(2,1)S(1)}, u32[]{:S(2)}, u32[]{:S(2)}) collective-permute-start(bf16[8,48,128]{2,1,0:T(8,128)(2,1)S(1)} %get-tuple-element.31), channel_id=1, source_target_pairs={{0,1},{1,0},{2,3},{3,2},{4,5},{5,4},{6,7},{7,6},{8,9},{9,8},{10,11... | collective-permute-start | bytes 294920 | tf_op jit(solution)/shard_map/ppermute | solution.py:323
  113.6 3.5 %collective-permute-start.1 = (bf16[8,48,128]{2,1,0:T(8,128)(2,1)S(1)}, bf16[8,48,128]{2,1,0:T(8,128)(2,1)S(1)}, u32[]{:S(2)}, u32[]{:S(2)}) collective-permute-start(bf16[8,48,128]{2,1,0:T(8,128)(2,1)S(1)} %get-tuple-element.30), channel_id=1, source_target_pairs={{0,2},{1,3},{2,0},{3,1},{4,6},{5,7},{6,4},{7,5},{8,10},{9,11},{10,... | collective-permute-start | bytes 294920 | tf_op jit(solution)/shard_map/ppermute | solution.py:323
  117.1 2.1 %collective-permute-start.2 = (bf16[8,48,128]{2,1,0:T(8,128)(2,1)}, bf16[8,48,128]{2,1,0:T(8,128)(2,1)S(1)}, u32[]{:S(2)}, u32[]{:S(2)}) collective-permute-start(bf16[8,48,128]{2,1,0:T(8,128)(2,1)} %get-tuple-element.29), channel_id=1, source_target_pairs={{0,3},{1,2},{2,1},{3,0},{4,7},{5,6},{6,5},{7,4},{8,11},{9,10},{10,... | collective-permute-start | bytes 294920 | tf_op jit(solution)/shard_map/ppermute | solution.py:323
  119.2 5.0 %collective-permute-start.3 = (bf16[8,48,128]{2,1,0:T(8,128)(2,1)}, bf16[8,48,128]{2,1,0:T(8,128)(2,1)S(1)}, u32[]{:S(2)}, u32[]{:S(2)}) collective-permute-start(bf16[8,48,128]{2,1,0:T(8,128)(2,1)} %get-tuple-element.28), channel_id=1, source_target_pairs={{0,4},{1,5},{2,6},{3,7},{4,0},{5,1},{6,2},{7,3},{8,12},{9,13},{10,... | collective-permute-start | bytes 294920 | tf_op jit(solution)/shard_map/ppermute | solution.py:323
  124.2 2.1 %collective-permute-start.4 = (bf16[8,48,128]{2,1,0:T(8,128)(2,1)}, bf16[8,48,128]{2,1,0:T(8,128)(2,1)S(1)}, u32[]{:S(2)}, u32[]{:S(2)}) collective-permute-start(bf16[8,48,128]{2,1,0:T(8,128)(2,1)} %get-tuple-element.27), channel_id=1, source_target_pairs={{0,5},{1,4},{2,7},{3,6},{4,1},{5,0},{6,3},{7,2},{8,13},{9,12},{10,... | collective-permute-start | bytes 294920 | tf_op jit(solution)/shard_map/ppermute | solution.py:323
  126.3 4.8 %collective-permute-start.5 = (bf16[8,48,128]{2,1,0:T(8,128)(2,1)}, bf16[8,48,128]{2,1,0:T(8,128)(2,1)}, u32[]{:S(2)}, u32[]{:S(2)}) collective-permute-start(bf16[8,48,128]{2,1,0:T(8,128)(2,1)} %get-tuple-element.26), channel_id=1, source_target_pairs={{0,6},{1,7},{2,4},{3,5},{4,2},{5,3},{6,0},{7,1},{8,14},{9,15},{10,... | collective-permute-start | bytes 294920 | tf_op jit(solution)/shard_map/ppermute | solution.py:323
  131.1 1.9 %collective-permute-start.6 = (bf16[8,48,128]{2,1,0:T(8,128)(2,1)}, bf16[8,48,128]{2,1,0:T(8,128)(2,1)}, u32[]{:S(2)}, u32[]{:S(2)}) collective-permute-start(bf16[8,48,128]{2,1,0:T(8,128)(2,1)} %get-tuple-element.25), channel_id=1, source_target_pairs={{0,7},{1,6},{2,5},{3,4},{4,3},{5,2},{6,1},{7,0},{8,15},{9,14},{10,... | collective-permute-start | bytes 294920 | tf_op jit(solution)/shard_map/ppermute | solution.py:323
  133.1 18.8 %all-to-all-done.2 = bf16[512,2,384]{2,1,0:T(2,128)(2,1)} async-done(((bf16[512,2,384]{2,1,0:T(2,128)(2,1)}), bf16[512,2,384]{2,1,0:T(2,128)(2,1)}, u32[]{:S(2)}, u32[]{:S(2)}) %all-to-all-start.2) | async-done | bytes 786464 | tf_op jit(solution)/shard_map/all_to_all | solution.py:330
  151.9 2.3 %reshape.164.spectrum_ref = bf16[1024,384]{1,0:T(8,128)(2,1)S(1)} reshape(bf16[512,2,384]{2,1,0:T(2,128)(2,1)} %all-to-all-done.2) | data formatting | bytes 1572864 | tf_op jit(solution)/shard_map/reshape | solution.py:333
  154.2 3.1 %shard_map.103 = bf16[8,48,1024]{2,1,0:T(8,128)(2,1)} custom-call(s32[8]{0:T(128)S(1)} %iota_xor_fusion.place_ref, bf16[1024,384]{1,0:T(8,128)(2,1)S(1)} %reshape.164.spectrum_ref, bf16[1024,1024]{1,0:T(8,128)(2,1)S(1)} %copy-done.2, bf16[8,48,128]{2,1,0:T(8,128)(2,1)S(1)} %get-tuple-element.32.refs_0_, ...), custom_call_target="tpu_custom_call" | custom-call | flops 800000000 | bytes 4000000 | tf_op jit(solution)/shard_map/pallas_call | solution.py:287
  (40 shorter events, 4.3 us)
Async XLA Ops:
  0.0 17.6 %all-to-all-start = ((bf16[8,128,384]{2,1,0:T(8,128)(2,1)}), bf16[8,128,384]{2,1,0:T(8,128)(2,1)S(1)}, u32[]{:S(2)}, u32[]{:S(2)}) async-start(bf16[8,128,384]{2,1,0:T(8,128)(2,1)} %param.10), calls=%async_computation | async-start | bytes 1572864 | tf_op jit(solution)/shard_map/all_to_all | solution.py:309
  17.6 1.6 %copy-start.3 = (bf16[1024,1024]{1,0:T(8,128)(2,1)S(1)}, bf16[1024,1024]{1,0:T(8,128)(2,1)}, u32[]{:S(2)}) copy-start(bf16[1024,1024]{1,0:T(8,128)(2,1)} %constant.74.clone.table_ref) | copy-start | bytes 6291460
  19.2 26.2 %copy-start.11 = (f32[512]{0:T(512)S(1)}, f32[512]{0:T(512)}, u32[]{:S(2)}) copy-start(f32[512]{0:T(512)} %constant.78.clone) | copy-start | bytes 6148
  19.2 26.9 %copy-start.10 = (f32[2,512]{1,0:T(2,128)S(1)}, f32[2,512]{1,0:T(2,128)}, u32[]{:S(2)}) copy-start(f32[2,512]{1,0:T(2,128)} %constant.77.clone) | copy-start | bytes 12292
  19.2 27.6 %copy-start = (bf16[1024,1024]{1,0:T(8,128)(2,1)S(1)}, bf16[1024,1024]{1,0:T(8,128)(2,1)}, u32[]{:S(2)}) copy-start(bf16[1024,1024]{1,0:T(8,128)(2,1)} %constant.75.clone.table_ref) | copy-start | bytes 6291460
  19.2 27.6 %copy-start.4 = (f32[2,512]{1,0:T(2,128)S(1)}, f32[2,512]{1,0:T(2,128)}, u32[]{:S(2)}) copy-start(f32[2,512]{1,0:T(2,128)} %constant.76.clone.cos_ref) | copy-start | bytes 12292
  19.2 27.6 %copy-start.5 = (f32[1,512]{1,0:T(1,128)S(1)}, f32[1,512]{1,0:T(1,128)}, u32[]{:S(2)}) copy-start(f32[1,512]{1,0:T(1,128)} %constant.81.weights_ref) | copy-start | bytes 6148
  22.2 66.5 %all-to-all-start.1 = ((bf16[512,2,384]{2,1,0:T(2,128)(2,1)}), bf16[512,2,384]{2,1,0:T(2,128)(2,1)}, u32[]{:S(2)}, u32[]{:S(2)}) async-start(bf16[512,2,384]{2,1,0:T(2,128)(2,1)} %bitcast.3), calls=%async_computation.1 | async-start | bytes 1572864 | tf_op jit(solution)/shard_map/all_to_all | solution.py:315
  49.9 1.3 copy-start.1
  51.3 0.8 copy-start.7
  53.7 35.1 %copy-start.6 = (f32[512,384]{1,0:T(8,128)S(1)}, f32[512,384]{1,0:T(8,128)}, u32[]{:S(2)}) copy-start(f32[512,384]{1,0:T(8,128)} %gain_ref.1) | copy-start | bytes 2359300
  53.7 35.1 %copy-start.8 = (bf16[512,512]{1,0:T(8,128)(2,1)S(1)}, bf16[512,512]{1,0:T(8,128)(2,1)}, u32[]{:S(2)}) copy-start(bf16[512,512]{1,0:T(8,128)(2,1)} %copy-done.7) | copy-start | bytes 1572868
  95.2 13.2 %copy-start.9 = (bf16[8,128,384]{2,1,0:T(8,128)(2,1)S(1)}, bf16[8,128,384]{2,1,0:T(8,128)(2,1)}, u32[]{:S(2)}) copy-start(bf16[8,128,384]{2,1,0:T(8,128)(2,1)} %param.10) | copy-start | bytes 2359300
  95.2 56.7 %all-to-all-start.2 = ((bf16[512,2,384]{2,1,0:T(2,128)(2,1)}), bf16[512,2,384]{2,1,0:T(2,128)(2,1)}, u32[]{:S(2)}, u32[]{:S(2)}) async-start(bf16[512,2,384]{2,1,0:T(2,128)(2,1)} %bitcast.14), calls=%async_computation.2 | async-start | bytes 1572864 | tf_op jit(solution)/shard_map/all_to_all | solution.py:330
  108.4 45.8 %copy-start.2 = (bf16[1024,1024]{1,0:T(8,128)(2,1)S(1)}, bf16[1024,1024]{1,0:T(8,128)(2,1)}, u32[]{:S(2)}) copy-start(bf16[1024,1024]{1,0:T(8,128)(2,1)} %copy-done.1) | copy-start | bytes 6291460
  111.6 14.7 %collective-permute-start = (bf16[8,48,128]{2,1,0:T(8,128)(2,1)S(1)}, bf16[8,48,128]{2,1,0:T(8,128)(2,1)S(1)}, u32[]{:S(2)}, u32[]{:S(2)}) collective-permute-start(bf16[8,48,128]{2,1,0:T(8,128)(2,1)S(1)} %get-tuple-element.31), channel_id=1, source_target_pairs={{0,1},{1,0},{2,3},{3,2},{4,5},{5,4},{6,7},{7,6},{8,9},{9,8},{10,11... | collective-permute-start | bytes 294920 | tf_op jit(solution)/shard_map/ppermute | solution.py:323
  113.6 17.5 %collective-permute-start.1 = (bf16[8,48,128]{2,1,0:T(8,128)(2,1)S(1)}, bf16[8,48,128]{2,1,0:T(8,128)(2,1)S(1)}, u32[]{:S(2)}, u32[]{:S(2)}) collective-permute-start(bf16[8,48,128]{2,1,0:T(8,128)(2,1)S(1)} %get-tuple-element.30), channel_id=1, source_target_pairs={{0,2},{1,3},{2,0},{3,1},{4,6},{5,7},{6,4},{7,5},{8,10},{9,11},{10,... | collective-permute-start | bytes 294920 | tf_op jit(solution)/shard_map/ppermute | solution.py:323
  117.1 37.1 %collective-permute-start.2 = (bf16[8,48,128]{2,1,0:T(8,128)(2,1)}, bf16[8,48,128]{2,1,0:T(8,128)(2,1)S(1)}, u32[]{:S(2)}, u32[]{:S(2)}) collective-permute-start(bf16[8,48,128]{2,1,0:T(8,128)(2,1)} %get-tuple-element.29), channel_id=1, source_target_pairs={{0,3},{1,2},{2,1},{3,0},{4,7},{5,6},{6,5},{7,4},{8,11},{9,10},{10,... | collective-permute-start | bytes 294920 | tf_op jit(solution)/shard_map/ppermute | solution.py:323
  119.2 35.0 %collective-permute-start.3 = (bf16[8,48,128]{2,1,0:T(8,128)(2,1)}, bf16[8,48,128]{2,1,0:T(8,128)(2,1)S(1)}, u32[]{:S(2)}, u32[]{:S(2)}) collective-permute-start(bf16[8,48,128]{2,1,0:T(8,128)(2,1)} %get-tuple-element.28), channel_id=1, source_target_pairs={{0,4},{1,5},{2,6},{3,7},{4,0},{5,1},{6,2},{7,3},{8,12},{9,13},{10,... | collective-permute-start | bytes 294920 | tf_op jit(solution)/shard_map/ppermute | solution.py:323
  124.2 30.0 %collective-permute-start.4 = (bf16[8,48,128]{2,1,0:T(8,128)(2,1)}, bf16[8,48,128]{2,1,0:T(8,128)(2,1)S(1)}, u32[]{:S(2)}, u32[]{:S(2)}) collective-permute-start(bf16[8,48,128]{2,1,0:T(8,128)(2,1)} %get-tuple-element.27), channel_id=1, source_target_pairs={{0,5},{1,4},{2,7},{3,6},{4,1},{5,0},{6,3},{7,2},{8,13},{9,12},{10,... | collective-permute-start | bytes 294920 | tf_op jit(solution)/shard_map/ppermute | solution.py:323
  126.3 27.9 %collective-permute-start.5 = (bf16[8,48,128]{2,1,0:T(8,128)(2,1)}, bf16[8,48,128]{2,1,0:T(8,128)(2,1)}, u32[]{:S(2)}, u32[]{:S(2)}) collective-permute-start(bf16[8,48,128]{2,1,0:T(8,128)(2,1)} %get-tuple-element.26), channel_id=1, source_target_pairs={{0,6},{1,7},{2,4},{3,5},{4,2},{5,3},{6,0},{7,1},{8,14},{9,15},{10,... | collective-permute-start | bytes 294920 | tf_op jit(solution)/shard_map/ppermute | solution.py:323
  131.1 23.1 %collective-permute-start.6 = (bf16[8,48,128]{2,1,0:T(8,128)(2,1)}, bf16[8,48,128]{2,1,0:T(8,128)(2,1)}, u32[]{:S(2)}, u32[]{:S(2)}) collective-permute-start(bf16[8,48,128]{2,1,0:T(8,128)(2,1)} %get-tuple-element.25), channel_id=1, source_target_pairs={{0,7},{1,6},{2,5},{3,4},{4,3},{5,2},{6,1},{7,0},{8,15},{9,14},{10,... | collective-permute-start | bytes 294920 | tf_op jit(solution)/shard_map/ppermute | solution.py:323

commit v3 on v2

v3 whole, which is shorter than its diff:
```python
import math

import jax
import jax.numpy as jnp
import numpy as np
from jax import lax
from jax.experimental import pallas as pl
from jax.experimental.pallas import tpu as pltpu
from jax.sharding import PartitionSpec as P

NLAT = 512
EMBED = 384
NLON = 1024
DEGREES = 512
MODES = 512
VMEM_LIMIT = 20 * 1024 * 1024


def grid_points():
    theta = math.pi * (np.arange(NLAT, dtype=np.float64) + 0.5) / NLAT
    harmonic = np.arange(1, NLAT // 2 + 1, dtype=np.float64)
    series = np.sum(
        np.cos(2.0 * harmonic[None, :] * theta[:, None]) / (4.0 * harmonic * harmonic - 1.0),
        axis=1,
    )
    weights = 2.0 / NLAT * (1.0 - 2.0 * series)
    return theta, weights


def order_starts():
    return np.array(
        [
            0.5 * (math.lgamma(m + 1.5) - math.lgamma(1.5) - math.lgamma(m + 1.0) - math.log(2.0))
            / math.log(2.0)
            for m in range(MODES)
        ]
    )


def dft_tables():
    phase = np.arange(MODES)[:, None] * np.arange(NLON)[None, :] % NLON
    angle = 2.0 * math.pi / NLON * phase
    parts = np.stack([np.cos(angle), -np.sin(angle)], axis=1)
    factor = np.where(np.arange(MODES) == 0, 1.0, 2.0)[:, None, None]
    forward = (parts / NLON).reshape(2, MODES // 2, 2, NLON).transpose(0, 2, 1, 3)
    forward = forward.reshape(2 * MODES, NLON)
    inverse = (parts * factor).transpose(1, 0, 2).reshape(2 * MODES, NLON)
    return forward.astype(jnp.bfloat16), inverse.astype(jnp.bfloat16)


def pair_weight(channel_mix):
    real_part = channel_mix[0]
    imag_part = channel_mix[1]
    upper = jnp.concatenate([real_part, imag_part], axis=1)
    lower = jnp.concatenate([-imag_part, real_part], axis=1)
    return jnp.concatenate([upper, lower], axis=0)


def permuted_latitudes():
    high, a, low = np.meshgrid(np.arange(4), np.arange(8), np.arange(16), indexing="ij")
    return ((16 * high + low) * 8 + a).reshape(-1)


def hold_kernel(table_ref, out_ref):
    out_ref[...] = table_ref[...]


def hold(table):
    vmem = pl.BlockSpec(memory_space=pltpu.VMEM)
    return pl.pallas_call(
        hold_kernel,
        out_shape=jax.ShapeDtypeStruct(table.shape, table.dtype),
        in_specs=[vmem],
        out_specs=vmem,
        cost_estimate=pl.CostEstimate(flops=0, bytes_accessed=4_000_000, transcendentals=0),
        compiler_params=pltpu.CompilerParams(vmem_limit_bytes=VMEM_LIMIT),
    )(table)


def transform_kernel(
    weights_ref, grid_ref, gain_ref, table_ref, out_ref, normed_ref, wide_ref, narrow_ref, out_sems
):
    row = lax.axis_index("lat") * 8 + lax.axis_index("chan")
    spot = lax.broadcasted_iota(jnp.int32, (4, 128), 0) * 128
    spot = spot + lax.broadcasted_iota(jnp.int32, (4, 128), 1)
    share = jnp.sum(jnp.where(spot == row, weights_ref[...], 0.0), axis=1, keepdims=True)
    share = jnp.sum(share, axis=0, keepdims=True)
    gain = gain_ref[...]
    for piece in range(8):
        rows = slice(128 * piece, 128 * piece + 128)
        values = grid_ref[rows, :].astype(jnp.float32)
        mean_value = jnp.mean(values, axis=1, keepdims=True)
        centered = values - mean_value
        variance = jnp.mean(centered * centered, axis=1, keepdims=True)
        normed_ref[rows, :] = (centered * lax.rsqrt(variance + 1e-05) * gain).astype(jnp.bfloat16)
    results = []
    for half in range(2):
        spectrum = jnp.dot(
            table_ref[512 * half : 512 * half + 512, :],
            normed_ref[...],
            preferred_element_type=jnp.float32,
        )
        spectrum = spectrum * share
        first = 1536 * half
        for r in range(2):
            for t in range(3):
                wide_ref[pl.ds(first + 2 * t + r, 256, stride=6), :] = spectrum[
                    256 * r : 256 * r + 256, 128 * t : 128 * t + 128
                ]
        rows = slice(first, first + 1536)
        narrow_ref[rows, :] = wide_ref[rows, :].astype(jnp.bfloat16)
        results.append(
            pltpu.make_async_copy(narrow_ref.at[rows], out_ref.at[rows], out_sems.at[half])
        )
        results[half].start()
    for half in range(2):
        results[half].wait()


def transform(weights, grid, gain, table):
    vmem = pl.BlockSpec(memory_space=pltpu.VMEM)
    return pl.pallas_call(
        transform_kernel,
        out_shape=jax.ShapeDtypeStruct((6 * MODES, 128), jnp.bfloat16),
        in_specs=[vmem] * 4,
        out_specs=pl.BlockSpec(memory_space=pltpu.MemorySpace.HBM),
        scratch_shapes=[
            pltpu.VMEM((NLON, EMBED), jnp.bfloat16),
            pltpu.VMEM((6 * MODES, 128), jnp.float32),
            pltpu.VMEM((6 * MODES, 128), jnp.bfloat16),
            pltpu.SemaphoreType.DMA((2,)),
        ],
        cost_estimate=pl.CostEstimate(
            flops=800_000_000, bytes_accessed=4_000_000, transcendentals=1024
        ),
        compiler_params=pltpu.CompilerParams(vmem_limit_bytes=VMEM_LIMIT),
    )(weights, grid, gain, table)


def spread_rows(source_ref, wide_ref, pieces_ref):
    wide_ref[...] = source_ref[...].astype(jnp.float32)
    for r in range(2):
        for t in range(3):
            pieces_ref[512 * r : 512 * r + 512, 128 * t : 128 * t + 128] = wide_ref[
                pl.ds(2 * t + r, 512, stride=6), :
            ].astype(jnp.bfloat16)


def pack_rows(rows):
    return rows.reshape(512, 3, 2, 128).transpose(0, 2, 1, 3).reshape(512, 2, EMBED)


def unpack_rows(pieces):
    return pieces.reshape(512, 2, 3, 128).transpose(0, 2, 1, 3).reshape(3072, 128)


def legendre_kernel(coef_ref, cos_ref, start_ref, exponent_ref, table_ref):
    cos_row = cos_ref[...]
    start = start_ref[...]

    def block(index, state):
        one, two, power = state
        base = index * 16
        parts = []
        for half in range(2):
            rows = []
            for k in range(8):
                level = base + 8 * half + k
                a = coef_ref[0, level]
                b = coef_ref[1, level]
                s = coef_ref[2, level]
                one, two = (a * cos_row) * one - b * two + s * start, one
                rows.append(one)
            parts.append(jnp.concatenate(rows, axis=0) * jnp.exp2(power))
            large = jnp.abs(one) > 1000.0
            factor = jnp.where(large, 2.0**-40, 1.0)
            power = power + jnp.where(large, 40.0, 0.0)
            one, two = one * factor, two * factor
        here = pl.ds(pl.multiple_of(base, 16), 16)
        table_ref[here, :] = jnp.concatenate(parts, axis=0).astype(jnp.bfloat16)
        return one, two, power

    zeros = jnp.zeros((1, NLAT), jnp.float32)
    lax.fori_loop(0, DEGREES // 16, block, (zeros, zeros, exponent_ref[...]))


def legendre_table(order):
    theta_row = grid_points()[0][permuted_latitudes()].reshape(1, NLAT)
    cos_row = jnp.asarray(np.cos(theta_row), jnp.float32)
    log_sine = jnp.asarray(np.log2(np.sin(theta_row)), jnp.float32)
    starts = jnp.asarray(order_starts(), jnp.float32)
    start = jnp.sum(jnp.where(jnp.arange(MODES) == order, starts, 0.0))
    m = order.astype(jnp.float32)
    log_start = start + m * log_sine
    exponent = jnp.floor(log_start)
    mantissa = jnp.exp2(log_start - exponent)
    level = jnp.arange(DEGREES, dtype=jnp.float32)
    denom = jnp.maximum(level * level - m * m, 1.0)
    above = level > m
    coef_a = jnp.where(above, jnp.sqrt(jnp.maximum(4.0 * level * level - 1.0, 1.0) / denom), 0.0)
    coef_b = jnp.sqrt(
        jnp.maximum((level - 1.0) * (level - 1.0) - m * m, 0.0)
        * (2.0 * level + 1.0)
        / (denom * jnp.maximum(2.0 * level - 3.0, 1.0))
    )
    coef_b = jnp.where(above, coef_b, 0.0)
    first = jnp.where(level == m, 1.0, 0.0)
    coefs = jnp.stack([coef_a, coef_b, first])
    vmem = pl.BlockSpec(memory_space=pltpu.VMEM)
    return pl.pallas_call(
        legendre_kernel,
        out_shape=jax.ShapeDtypeStruct((DEGREES, NLAT), jnp.bfloat16),
        in_specs=[pl.BlockSpec(memory_space=pltpu.SMEM)] + [vmem] * 3,
        out_specs=vmem,
        cost_estimate=pl.CostEstimate(
            flops=40_000_000, bytes_accessed=8_000_000, transcendentals=65536
        ),
        compiler_params=pltpu.CompilerParams(vmem_limit_bytes=VMEM_LIMIT),
    )(coefs, cos_row, mantissa, exponent)


def mix_kernel(
    arrived_ref,
    table_ref,
    gain_ref,
    weight_ref,
    spare_ref,
    out_ref,
    wide_ref,
    pieces_ref,
    field_ref,
    narrow_ref,
    out_sems,
):
    wide_ref[...] = arrived_ref[...].astype(jnp.float32)
    for r in range(2):
        for high in range(4):
            for a in range(8):
                rows = slice(512 * r + 128 * high + 16 * a, 512 * r + 128 * high + 16 * a + 16)
                for t in range(3):
                    first = 768 * high + 6 * a + 2 * t + r
                    pieces_ref[rows, 128 * t : 128 * t + 128] = wide_ref[
                        pl.ds(first, 16, stride=48), :
                    ].astype(jnp.bfloat16)
    gain = gain_ref[...]
    parts = []
    for r in range(2):
        coeffs = jnp.dot(
            table_ref[...],
            pieces_ref[512 * r : 512 * r + 512, :],
            preferred_element_type=jnp.float32,
        )
        parts.append((coeffs * gain).astype(jnp.bfloat16))
    scaled = jnp.concatenate(parts, axis=1)
    mixed = lax.dot_general(
        weight_ref[...], scaled, (((1,), (1,)), ((), ())), preferred_element_type=jnp.float32
    ).astype(jnp.bfloat16)
    lane = lax.broadcasted_iota(jnp.int32, (8, 128), 1)
    masks = {d: (lane & d) != 0 for d in (1, 2, 4, 8)}
    results = []
    for pair in range(2):
        field_ref[:, 256 * pair : 256 * pair + 256] = jnp.dot(
            mixed, table_ref[:, 256 * pair : 256 * pair + 256], preferred_element_type=jnp.float32
        )
    for high in range(4):
        columns = slice(128 * high, 128 * high + 128)

        def group(index, carry, high=high, columns=columns):
            rows = pl.multiple_of(index * 16, 16)
            halves = []
            for half in range(2):
                pieces = []
                for i in range(16):
                    piece = field_ref[pl.ds(48 * i + rows + 8 * half, 8), columns]
                    pieces.append(pltpu.roll(piece, i, 1) if i else piece)
                for d in (1, 2, 4, 8):
                    pieces = [
                        jnp.where(masks[d], pieces[(k + d) % 16], pieces[k]) for k in range(16)
                    ]
                halves.append([pieces[(16 - low) % 16] for low in range(16)])
            for low in range(16):
                both = jnp.concatenate([halves[0][low], halves[1][low]], axis=0)
                here = pl.ds(48 * (high * 16 + low) + rows, 16)
                narrow_ref[here, :] = both.astype(jnp.bfloat16)
            return carry

        lax.fori_loop(0, 3, group, 0)
        here = slice(768 * high, 768 * high + 768)
        results.append(
            pltpu.make_async_copy(narrow_ref.at[here], out_ref.at[here], out_sems.at[high])
        )
        results[high].start()
    for high in range(4):
        results[high].wait()


def mix_and_return(arrived, table, gain, weight, spare):
    vmem = pl.BlockSpec(memory_space=pltpu.VMEM)
    return pl.pallas_call(
        mix_kernel,
        out_shape=jax.ShapeDtypeStruct((6 * MODES, 128), jnp.bfloat16),
        in_specs=[vmem] * 4 + [pl.BlockSpec(memory_space=pltpu.MemorySpace.HBM)],
        out_specs=pl.BlockSpec(memory_space=pltpu.MemorySpace.HBM),
        input_output_aliases={4: 0},
        scratch_shapes=[
            pltpu.VMEM((6 * NLAT, 128), jnp.float32),
            pltpu.VMEM((2 * NLAT, EMBED), jnp.bfloat16),
            pltpu.VMEM((2 * EMBED, NLAT), jnp.float32),
            pltpu.VMEM((6 * MODES, 128), jnp.bfloat16),
            pltpu.SemaphoreType.DMA((4,)),
        ],
        cost_estimate=pl.CostEstimate(
            flops=1_400_000_000, bytes_accessed=4_000_000, transcendentals=0
        ),
        compiler_params=pltpu.CompilerParams(vmem_limit_bytes=VMEM_LIMIT),
    )(arrived, table, gain, weight, spare)


def gather_kernel(place_ref, table_ref, *refs):
    grid_refs, out_ref = refs[:8], refs[8]
    for k in range(8):
        columns = pl.ds(pl.multiple_of(place_ref[k] * 128, 128), 128)
        out_ref[:, :, columns] = grid_refs[k][...]


def gather(places, table, grids):
    vmem = pl.BlockSpec(memory_space=pltpu.VMEM)
    return pl.pallas_call(
        gather_kernel,
        out_shape=jax.ShapeDtypeStruct((8, 48, NLON), jnp.bfloat16),
        in_specs=[pl.BlockSpec(memory_space=pltpu.SMEM)] + [vmem] * 9,
        out_specs=vmem,
        cost_estimate=pl.CostEstimate(flops=0, bytes_accessed=6_000_000, transcendentals=0),
        compiler_params=pltpu.CompilerParams(vmem_limit_bytes=VMEM_LIMIT),
    )(places, table, *grids)


def restore_kernel(
    spectrum_ref,
    table_ref,
    grid_ref,
    out_ref,
    wide_ref,
    pieces_ref,
    field_ref,
    held_ref,
    narrow_ref,
    grid_sem,
    out_sems,
):
    grid_copy = pltpu.make_async_copy(grid_ref, held_ref, grid_sem)
    grid_copy.start()
    spread_rows(spectrum_ref, wide_ref, pieces_ref)
    field = lax.dot_general(
        pieces_ref[...],
        table_ref[...],
        (((0,), (0,)), ((), ())),
        preferred_element_type=jnp.float32,
    )
    for t in range(3):
        for s in range(8):
            columns = slice(128 * s, 128 * s + 128)
            field_ref[pl.ds(1152 * t + s, 128, stride=8), :] = field[128 * t : 128 * t + 128, columns]
            field_ref[pl.ds(1152 * t + 1024 + s, 16, stride=8), :] = field[
                128 * t : 128 * t + 16, columns
            ]
    turn = pl.multiple_of(lax.rem(lax.axis_index("lat"), 16) * 8, 8)
    grid_copy.wait()
    results = []
    for a in range(8):
        for t in range(3):
            first = 8 * (144 * t + 16 * a)
            piece = jnp.concatenate(
                [field_ref[pl.ds(first + turn + s, 16, stride=8), :] for s in range(8)], axis=1
            )
            rows = slice(16 * t, 16 * t + 16)
            own = held_ref[a, rows, :].astype(jnp.float32)
            narrow_ref[a, rows, :] = (own + piece).astype(jnp.bfloat16)
        results.append(pltpu.make_async_copy(narrow_ref.at[a], out_ref.at[a], out_sems.at[a]))
        results[a].start()
    for a in range(8):
        results[a].wait()


def restore(spectrum, table, grid):
    vmem = pl.BlockSpec(memory_space=pltpu.VMEM)
    return pl.pallas_call(
        restore_kernel,
        out_shape=jax.ShapeDtypeStruct((8, 48, NLON), jnp.bfloat16),
        in_specs=[vmem, vmem, pl.BlockSpec(memory_space=pltpu.MemorySpace.HBM)],
        out_specs=pl.BlockSpec(memory_space=pltpu.MemorySpace.HBM),
        input_output_aliases={2: 0},
        scratch_shapes=[
            pltpu.VMEM((6 * MODES, 128), jnp.float32),
            pltpu.VMEM((2 * MODES, EMBED), jnp.bfloat16),
            pltpu.VMEM((3 * 144 * 8, 128), jnp.float32),
            pltpu.VMEM((8, 48, NLON), jnp.bfloat16),
            pltpu.VMEM((8, 48, NLON), jnp.bfloat16),
            pltpu.SemaphoreType.DMA,
            pltpu.SemaphoreType.DMA((8,)),
        ],
        cost_estimate=pl.CostEstimate(
            flops=800_000_000, bytes_accessed=4_000_000, transcendentals=0
        ),
        compiler_params=pltpu.CompilerParams(vmem_limit_bytes=VMEM_LIMIT),
    )(spectrum, table, grid)


def mix_weight(channel_mix):
    paired = pair_weight(channel_mix).T.reshape(2, 24, 16, 2 * EMBED)
    return paired.transpose(2, 1, 0, 3).reshape(2 * EMBED, 2 * EMBED)


def on_device(grid_field, norm_gain, degree_gain, channel_mix):
    both = ("lat", "chan")
    place = lax.axis_index("chan")
    forward_dft, inverse_dft = dft_tables()
    own = lax.all_to_all(grid_field, "chan", split_axis=0, concat_axis=0, tiled=True)
    own = own.reshape(NLON, EMBED)
    weights = jnp.asarray(grid_points()[1].reshape(4, 128), jnp.float32)
    own, forward_dft = lax.optimization_barrier((own, hold(jnp.asarray(forward_dft))))
    rows = transform(weights, own, norm_gain.reshape(1, EMBED), forward_dft)
    spectrum = pack_rows(rows)
    spectrum, grid_later, channel_mix = lax.optimization_barrier(
        (spectrum, grid_field, channel_mix)
    )
    arrived = lax.all_to_all(spectrum, both, split_axis=0, concat_axis=0, tiled=True)
    legendre = legendre_table(lax.axis_index(both))
    weight = mix_weight(channel_mix)
    pieces = grid_later.transpose(0, 2, 1).reshape(8, 8, 48, 128).transpose(1, 0, 2, 3)
    grids = [lax.dynamic_index_in_dim(pieces, place ^ k, 0, keepdims=False) for k in range(8)]
    grids = [grids[0]] + [
        lax.ppermute(grids[k], "chan", [(i, i ^ k) for i in range(8)]) for k in range(1, 8)
    ]
    places = jnp.arange(8, dtype=jnp.int32) ^ place
    field = mix_and_return(unpack_rows(arrived), legendre, degree_gain, weight, rows)
    returned = lax.all_to_all(
        pack_rows(field), both, split_axis=0, concat_axis=0, tiled=True
    )
    table = jnp.asarray(inverse_dft)
    grid = gather(places, table, grids)
    block_out = restore(unpack_rows(returned), table, grid)
    return block_out.transpose(0, 2, 1)


def solution(mesh):
    return jax.shard_map(
        on_device,
        mesh=mesh,
        in_specs=(P("lat", "chan", None), P(), P(), P()),
        out_specs=P("lat", None, "chan"),
        check_vma=False,
    )
```

time: 160 us -> 153 us (0.956)
  local copies, waits for them, and re-layouts: 16.5 us -> 11.3 us
  starting transfers between devices: 62.1 us -> 57.9 us
  waiting for transfers between devices: 61.2 us -> 64.7 us
  Pallas kernels: 15.6 us -> 13.7 us
    all_to_all x1, waiting for transfers between devices: 18.8 us -> 11.9 us  [on_device(): lax.all_to_all(pack_rows(field), both, split_axis=0, concat_axis=0, tiled...]
    ppermute x7, waiting for transfers between devices: 0.02 us -> 6.63 us  [on_device(): lax.ppermute(grids[k], 'chan', [(i, i ^ k) for i in range(8)])]
    all_to_all x1, waiting for transfers between devices: 29.9 us -> 35.3 us  [on_device(): lax.all_to_all(spectrum, both, split_axis=0, concat_axis=0, tiled=True)]
    reshape x2 -> x1, local copies, waits for them, and re-layouts: 2.94 us -> 0.01 us  [on_device(): rows = transform(weights, own, norm_gain.reshape(1, EMBED), forward_dft)]
    all_to_all x1, starting transfers between devices: 13.2 us -> 10.8 us  [on_device(): lax.all_to_all(pack_rows(field), both, split_axis=0, concat_axis=0, tiled...]
    all_to_all x1, starting transfers between devices: 23.1 us -> 21.3 us  [on_device(): lax.all_to_all(spectrum, both, split_axis=0, concat_axis=0, tiled=True)]
    unnamed x24 -> x18, local copies, waits for them, and re-layouts: 3.74 us -> 2.16 us
    pallas_call x2 -> x4, Pallas kernels: 9.49 us -> 8.89 us  [the longest x1 4.32 us: mix_and_return(): pl.pallas_call(mix_kernel, out_shape=jax.ShapeDtypeStruct((6 * MODES, 128...]
  transfers between devices with their start and end apart: 10 -> 10, of which waited for: 3 -> 6; matrix products, arithmetic and copies ran while one was open for 9% -> 7% of each run, Pallas kernels for 2% -> 3%
where the time goes in v3:
time: 153 us; the launch traced here: 150 us
  waiting for transfers between devices  64.7 us (42%)
  starting transfers between devices  57.9 us (38%)
  Pallas kernels  13.7 us (9%)
  local copies, waits for them, and re-layouts  11.3 us (7%)
    all_to_all x1, waiting for transfers between devices, on_device(): lax.all_to_all(spectrum, both, split_axis=0, concat_axis=0, tiled=True)  35.3 us
    ppermute x7, starting transfers between devices, on_device(): lax.ppermute(grids[k], 'chan', [(i, i ^ k) for i in range(8)])  21.4 us
    all_to_all x1, starting transfers between devices, on_device(): lax.all_to_all(spectrum, both, split_axis=0, concat_axis=0, tiled=True)  21.3 us
    all_to_all x1, waiting for transfers between devices, on_device(): lax.all_to_all(pack_rows(field), both, split_axis=0, concat_axis=0, tiled...  11.9 us
    all_to_all x1, waiting for transfers between devices, on_device(): lax.all_to_all(grid_field, 'chan', split_axis=0, concat_axis=0, tiled=True)  10.9 us
    all_to_all x1, starting transfers between devices, on_device(): lax.all_to_all(pack_rows(field), both, split_axis=0, concat_axis=0, tiled...  10.8 us
    ppermute x7, waiting for transfers between devices, on_device(): lax.ppermute(grids[k], 'chan', [(i, i ^ k) for i in range(8)])  6.63 us
    all_to_all x1, starting transfers between devices, on_device(): lax.all_to_all(grid_field, 'chan', split_axis=0, concat_axis=0, tiled=True)  4.47 us
  transfers between devices with their start and end apart: 10, of which 6 were waited for; matrix products, arithmetic and copies ran while one was open for 7% of the time, Pallas kernels for 3%

profile of v3, /device:TPU:6, one launch (start us, length us, event | category | flops | bytes accessed | tf_op | source)
XLA Modules:
  0.0 149.6 jit_solution(10399790667785078634)
XLA Ops:
  0.0 4.5 %all-to-all-start = ((bf16[8,128,384]{2,1,0:T(8,128)(2,1)}), bf16[8,128,384]{2,1,0:T(8,128)(2,1)S(1)}, u32[]{:S(2)}, u32[]{:S(2)}) async-start(bf16[8,128,384]{2,1,0:T(8,128)(2,1)} %param.10), calls=%async_computation | async-start | bytes 1572864 | tf_op jit(solution)/shard_map/all_to_all | solution.py:418
  4.5 1.6 %copy-done.1 = bf16[1024,1024]{1,0:T(8,128)(2,1)S(1)} copy-done((bf16[1024,1024]{1,0:T(8,128)(2,1)S(1)}, bf16[1024,1024]{1,0:T(8,128)(2,1)}, u32[]{:S(2)}) %copy-start.1) | copy-done | bytes 2097176
  6.7 10.9 %all-to-all-done = bf16[8,128,384]{2,1,0:T(8,128)(2,1)S(1)} async-done(((bf16[8,128,384]{2,1,0:T(8,128)(2,1)}), bf16[8,128,384]{2,1,0:T(8,128)(2,1)S(1)}, u32[]{:S(2)}, u32[]{:S(2)}) %all-to-all-start) | async-done | bytes 786464 | tf_op jit(solution)/shard_map/all_to_all | solution.py:418
  17.7 2.5 %shard_map.101.spare_ref = bf16[3072,128]{1,0:T(8,128)(2,1)} custom-call(f32[4,128]{1,0:T(4,128)S(1)} %copy-done.3, bf16[1024,384]{1,0:T(8,128)(2,1)S(1)} %bitcast.53, f32[1,384]{1,0:T(1,128)S(1)} %reshape.158.gain_ref, bf16[1024,1024]{1,0:T(8,128)(2,1)S(1)} %shard_map.100.table_ref), custom_call_target="tpu_custom_call" | custom-call | flops 800000000 | bytes 4000000 | tf_op jit(solution)/shard_map/pallas_call | solution.py:122
  20.2 21.3 %all-to-all-start.1 = ((bf16[512,2,384]{2,1,0:T(2,128)(2,1)}), bf16[512,2,384]{2,1,0:T(2,128)(2,1)S(1)}, u32[]{:S(2)}, u32[]{:S(2)}) async-start(bf16[512,2,384]{2,1,0:T(2,128)(2,1)} %bitcast.3), calls=%async_computation.1 | async-start | bytes 1572864 | tf_op jit(solution)/shard_map/all_to_all | solution.py:427
  42.8 2.8 %shard_map.102.table_ref = bf16[512,512]{1,0:T(8,128)(2,1)S(1)} custom-call(f32[3,512]{1,0:T(4,128)S(1)} %pad_maximum_fusion.coef_ref, f32[1,512]{1,0:T(1,128)S(1)} %copy-done.2, f32[1,512]{1,0:T(1,128)S(1)} %get-tuple-element.26.start_ref, f32[1,512]{1,0:T(1,128)S(1)} %get-tuple-element.25.exponent_ref), custom_call_target="tpu_custom_call" | custom-call | flops 40000000 | bytes 8000000 | tf_op jit(solution)/shard_map/pallas_call | solution.py:210
  46.2 2.2 %copy.24 = bf16[16,24,2,768]{3,2,1,0:T(2,128)(2,1)} copy(bf16[16,24,2,768]{3,0,1,2:T(8,128)(2,1)S(1)} %bitcast.55) | data formatting | bytes 2359296 | tf_op jit(solution)/shard_map/transpose | solution.py:411
  48.4 3.0 %reshape.164.weight_ref = bf16[768,768]{1,0:T(8,128)(2,1)S(1)} reshape(bf16[16,24,2,768]{3,2,1,0:T(2,128)(2,1)} %copy.24) | data formatting | bytes 2359296 | tf_op jit(solution)/shard_map/reshape | solution.py:411
  51.4 35.3 %all-to-all-done.1 = bf16[512,2,384]{2,1,0:T(2,128)(2,1)S(1)} async-done(((bf16[512,2,384]{2,1,0:T(2,128)(2,1)}), bf16[512,2,384]{2,1,0:T(2,128)(2,1)S(1)}, u32[]{:S(2)}, u32[]{:S(2)}) %all-to-all-start.1) | async-done | bytes 786464 | tf_op jit(solution)/shard_map/all_to_all | solution.py:427
  86.7 4.3 %shard_map.103 = bf16[3072,128]{1,0:T(8,128)(2,1)} custom-call(bf16[3072,128]{1,0:T(8,128)(2,1)S(1)} %bitcast.54, bf16[512,512]{1,0:T(8,128)(2,1)S(1)} %shard_map.102.table_ref, f32[512,384]{1,0:T(8,128)S(1)} %copy-done.4, bf16[768,768]{1,0:T(8,128)(2,1)S(1)} %reshape.164.weight_ref, ...), custom_call_target="tpu_custom_call", output_to_operand_aliasing={{}: (4, {})} | custom-call | flops 1400000000 | bytes 4000000 | tf_op jit(solution)/shard_map/pallas_call | solution.py:299
  91.0 10.8 %all-to-all-start.2 = ((bf16[512,2,384]{2,1,0:T(2,128)(2,1)}), bf16[512,2,384]{2,1,0:T(2,128)(2,1)S(1)}, u32[]{:S(2)}, u32[]{:S(2)}) async-start(bf16[512,2,384]{2,1,0:T(2,128)(2,1)} %bitcast.14), calls=%async_computation.2 | async-start | bytes 1572864 | tf_op jit(solution)/shard_map/all_to_all | solution.py:437
  101.9 2.3 %copy.25 = bf16[8,128,384]{1,2,0:T(8,128)(2,1)} copy(bf16[8,128,384]{2,1,0:T(8,128)(2,1)} %param.10) | data formatting | bytes 1572864 | tf_op jit(solution)/shard_map/optimization_barrier | solution.py:424
  105.4 2.1 %collective-permute-start = (bf16[8,48,128]{2,1,0:T(8,128)(2,1)S(1)}, bf16[8,48,128]{2,1,0:T(8,128)(2,1)S(1)}, u32[]{:S(2)}, u32[]{:S(2)}) collective-permute-start(bf16[8,48,128]{2,1,0:T(8,128)(2,1)S(1)} %get-tuple-element.21), channel_id=1, source_target_pairs={{0,1},{1,0},{2,3},{3,2},{4,5},{5,4},{6,7},{7,6},{8,9},{9,8},{10,11... | collective-permute-start | bytes 294920 | tf_op jit(solution)/shard_map/ppermute | solution.py:433
  107.5 3.5 %collective-permute-start.1 = (bf16[8,48,128]{2,1,0:T(8,128)(2,1)S(1)}, bf16[8,48,128]{2,1,0:T(8,128)(2,1)S(1)}, u32[]{:S(2)}, u32[]{:S(2)}) collective-permute-start(bf16[8,48,128]{2,1,0:T(8,128)(2,1)S(1)} %get-tuple-element.20), channel_id=1, source_target_pairs={{0,2},{1,3},{2,0},{3,1},{4,6},{5,7},{6,4},{7,5},{8,10},{9,11},{10,... | collective-permute-start | bytes 294920 | tf_op jit(solution)/shard_map/ppermute | solution.py:433
  110.9 2.1 %collective-permute-start.2 = (bf16[8,48,128]{2,1,0:T(8,128)(2,1)S(1)}, bf16[8,48,128]{2,1,0:T(8,128)(2,1)S(1)}, u32[]{:S(2)}, u32[]{:S(2)}) collective-permute-start(bf16[8,48,128]{2,1,0:T(8,128)(2,1)S(1)} %get-tuple-element.19), channel_id=1, source_target_pairs={{0,3},{1,2},{2,1},{3,0},{4,7},{5,6},{6,5},{7,4},{8,11},{9,10},{10,... | collective-permute-start | bytes 294920 | tf_op jit(solution)/shard_map/ppermute | solution.py:433
  113.0 5.0 %collective-permute-start.3 = (bf16[8,48,128]{2,1,0:T(8,128)(2,1)S(1)}, bf16[8,48,128]{2,1,0:T(8,128)(2,1)S(1)}, u32[]{:S(2)}, u32[]{:S(2)}) collective-permute-start(bf16[8,48,128]{2,1,0:T(8,128)(2,1)S(1)} %get-tuple-element.18), channel_id=1, source_target_pairs={{0,4},{1,5},{2,6},{3,7},{4,0},{5,1},{6,2},{7,3},{8,12},{9,13},{10,... | collective-permute-start | bytes 294920 | tf_op jit(solution)/shard_map/ppermute | solution.py:433
  118.0 2.1 %collective-permute-start.4 = (bf16[8,48,128]{2,1,0:T(8,128)(2,1)S(1)}, bf16[8,48,128]{2,1,0:T(8,128)(2,1)S(1)}, u32[]{:S(2)}, u32[]{:S(2)}) collective-permute-start(bf16[8,48,128]{2,1,0:T(8,128)(2,1)S(1)} %get-tuple-element.17), channel_id=1, source_target_pairs={{0,5},{1,4},{2,7},{3,6},{4,1},{5,0},{6,3},{7,2},{8,13},{9,12},{10,... | collective-permute-start | bytes 294920 | tf_op jit(solution)/shard_map/ppermute | solution.py:433
  120.2 4.8 %collective-permute-start.5 = (bf16[8,48,128]{2,1,0:T(8,128)(2,1)S(1)}, bf16[8,48,128]{2,1,0:T(8,128)(2,1)S(1)}, u32[]{:S(2)}, u32[]{:S(2)}) collective-permute-start(bf16[8,48,128]{2,1,0:T(8,128)(2,1)S(1)} %get-tuple-element.16), channel_id=1, source_target_pairs={{0,6},{1,7},{2,4},{3,5},{4,2},{5,3},{6,0},{7,1},{8,14},{9,15},{10,... | collective-permute-start | bytes 294920 | tf_op jit(solution)/shard_map/ppermute | solution.py:433
  125.0 1.9 %collective-permute-start.6 = (bf16[8,48,128]{2,1,0:T(8,128)(2,1)S(1)}, bf16[8,48,128]{2,1,0:T(8,128)(2,1)S(1)}, u32[]{:S(2)}, u32[]{:S(2)}) collective-permute-start(bf16[8,48,128]{2,1,0:T(8,128)(2,1)S(1)} %get-tuple-element.15), channel_id=1, source_target_pairs={{0,7},{1,6},{2,5},{3,4},{4,3},{5,2},{6,1},{7,0},{8,15},{9,14},{10,... | collective-permute-start | bytes 294920 | tf_op jit(solution)/shard_map/ppermute | solution.py:433
  127.1 3.0 %collective-permute-done.5.refs_6_ = bf16[8,48,128]{2,1,0:T(8,128)(2,1)S(1)} collective-permute-done((bf16[8,48,128]{2,1,0:T(8,128)(2,1)S(1)}, bf16[8,48,128]{2,1,0:T(8,128)(2,1)S(1)}, u32[]{:S(2)}, u32[]{:S(2)}) %collective-permute-start.5) | collective-permute-done | bytes 98336 | tf_op jit(solution)/shard_map/ppermute | solution.py:433
  130.1 3.5 %collective-permute-done.6.refs_7_ = bf16[8,48,128]{2,1,0:T(8,128)(2,1)S(1)} collective-permute-done((bf16[8,48,128]{2,1,0:T(8,128)(2,1)S(1)}, bf16[8,48,128]{2,1,0:T(8,128)(2,1)S(1)}, u32[]{:S(2)}, u32[]{:S(2)}) %collective-permute-start.6) | collective-permute-done | bytes 98336 | tf_op jit(solution)/shard_map/ppermute | solution.py:433
  133.6 1.6 %shard_map.104.grid_ref = bf16[8,48,1024]{2,1,0:T(8,128)(2,1)} custom-call(s32[8]{0:T(128)S(1)} %iota_xor_fusion.place_ref, bf16[1024,1024]{1,0:T(8,128)(2,1)S(1)} %copy-done, bf16[8,48,128]{2,1,0:T(8,128)(2,1)S(1)} %get-tuple-element.22.refs_0_, bf16[8,48,128]{2,1,0:T(8,128)(2,1)S(1)} %collective-permute-done.refs_1_, ...), custom_call_target="tpu_custom_call" | custom-call | bytes 6000000 | tf_op jit(solution)/shard_map/pallas_call | solution.py:328
  135.2 11.9 %all-to-all-done.2 = bf16[512,2,384]{2,1,0:T(2,128)(2,1)S(1)} async-done(((bf16[512,2,384]{2,1,0:T(2,128)(2,1)}), bf16[512,2,384]{2,1,0:T(2,128)(2,1)S(1)}, u32[]{:S(2)}, u32[]{:S(2)}) %all-to-all-start.2) | async-done | bytes 786464 | tf_op jit(solution)/shard_map/all_to_all | solution.py:437
  147.1 2.3 %shard_map.105 = bf16[8,48,1024]{2,1,0:T(8,128)(2,1)} custom-call(bf16[3072,128]{1,0:T(8,128)(2,1)S(1)} %bitcast.52, bf16[1024,1024]{1,0:T(8,128)(2,1)S(1)} %copy-done, bf16[8,48,1024]{2,1,0:T(8,128)(2,1)} %shard_map.104.grid_ref), custom_call_target="tpu_custom_call", output_to_operand_aliasing={{}: (2, {})} | custom-call | flops 800000000 | bytes 4000000 | tf_op jit(solution)/shard_map/pallas_call | solution.py:387
  (34 shorter events, 4.0 us)
Async XLA Ops:
  0.0 17.6 %all-to-all-start = ((bf16[8,128,384]{2,1,0:T(8,128)(2,1)}), bf16[8,128,384]{2,1,0:T(8,128)(2,1)S(1)}, u32[]{:S(2)}, u32[]{:S(2)}) async-start(bf16[8,128,384]{2,1,0:T(8,128)(2,1)} %param.10), calls=%async_computation | async-start | bytes 1572864 | tf_op jit(solution)/shard_map/all_to_all | solution.py:418
  4.5 1.6 %copy-start.1 = (bf16[1024,1024]{1,0:T(8,128)(2,1)S(1)}, bf16[1024,1024]{1,0:T(8,128)(2,1)}, u32[]{:S(2)}) copy-start(bf16[1024,1024]{1,0:T(8,128)(2,1)} %constant.75.clone.table_ref) | copy-start | bytes 6291460
  6.1 0.7 copy-start.7
  6.1 11.6 %copy-start.3 = (f32[4,128]{1,0:T(4,128)S(1)}, f32[4,128]{1,0:T(4,128)}, u32[]{:S(2)}) copy-start(f32[4,128]{1,0:T(4,128)} %constant.74.clone.weights_ref) | copy-start | bytes 6148
  17.6 23.9 %copy-start.8 = (f32[512]{0:T(512)S(1)}, f32[512]{0:T(512)}, u32[]{:S(2)}) copy-start(f32[512]{0:T(512)} %constant.78.clone) | copy-start | bytes 6148
  17.6 24.5 %copy-start.6 = (f32[1,512]{1,0:T(1,128)S(1)}, f32[1,512]{1,0:T(1,128)}, u32[]{:S(2)}) copy-start(f32[1,512]{1,0:T(1,128)} %constant.77.clone) | copy-start | bytes 6148
  17.6 25.2 %copy-start.2 = (f32[1,512]{1,0:T(1,128)S(1)}, f32[1,512]{1,0:T(1,128)}, u32[]{:S(2)}) copy-start(f32[1,512]{1,0:T(1,128)} %constant.76.clone.cos_ref) | copy-start | bytes 6148
  17.6 28.0 %copy-start.5 = (bf16[2,384,384]{2,1,0:T(8,128)(2,1)S(1)}, bf16[2,384,384]{2,1,0:T(8,128)(2,1)}, u32[]{:S(2)}) copy-start(bf16[2,384,384]{2,1,0:T(8,128)(2,1)} %param.13) | copy-start | bytes 1769476
  20.2 66.5 %all-to-all-start.1 = ((bf16[512,2,384]{2,1,0:T(2,128)(2,1)}), bf16[512,2,384]{2,1,0:T(2,128)(2,1)S(1)}, u32[]{:S(2)}, u32[]{:S(2)}) async-start(bf16[512,2,384]{2,1,0:T(2,128)(2,1)} %bitcast.3), calls=%async_computation.1 | async-start | bytes 1572864 | tf_op jit(solution)/shard_map/all_to_all | solution.py:427
  46.2 40.5 %copy-start.4 = (f32[512,384]{1,0:T(8,128)S(1)}, f32[512,384]{1,0:T(8,128)}, u32[]{:S(2)}) copy-start(f32[512,384]{1,0:T(8,128)} %gain_ref.1) | copy-start | bytes 2359300
  91.0 42.6 %copy-start = (bf16[1024,1024]{1,0:T(8,128)(2,1)S(1)}, bf16[1024,1024]{1,0:T(8,128)(2,1)}, u32[]{:S(2)}) copy-start(bf16[1024,1024]{1,0:T(8,128)(2,1)} %constant.79.clone.table_ref) | copy-start | bytes 6291460
  91.0 56.1 %all-to-all-start.2 = ((bf16[512,2,384]{2,1,0:T(2,128)(2,1)}), bf16[512,2,384]{2,1,0:T(2,128)(2,1)S(1)}, u32[]{:S(2)}, u32[]{:S(2)}) async-start(bf16[512,2,384]{2,1,0:T(2,128)(2,1)} %bitcast.14), calls=%async_computation.2 | async-start | bytes 1572864 | tf_op jit(solution)/shard_map/all_to_all | solution.py:437
  105.4 14.7 %collective-permute-start = (bf16[8,48,128]{2,1,0:T(8,128)(2,1)S(1)}, bf16[8,48,128]{2,1,0:T(8,128)(2,1)S(1)}, u32[]{:S(2)}, u32[]{:S(2)}) collective-permute-start(bf16[8,48,128]{2,1,0:T(8,128)(2,1)S(1)} %get-tuple-element.21), channel_id=1, source_target_pairs={{0,1},{1,0},{2,3},{3,2},{4,5},{5,4},{6,7},{7,6},{8,9},{9,8},{10,11... | collective-permute-start | bytes 294920 | tf_op jit(solution)/shard_map/ppermute | solution.py:433
  107.5 17.5 %collective-permute-start.1 = (bf16[8,48,128]{2,1,0:T(8,128)(2,1)S(1)}, bf16[8,48,128]{2,1,0:T(8,128)(2,1)S(1)}, u32[]{:S(2)}, u32[]{:S(2)}) collective-permute-start(bf16[8,48,128]{2,1,0:T(8,128)(2,1)S(1)} %get-tuple-element.20), channel_id=1, source_target_pairs={{0,2},{1,3},{2,0},{3,1},{4,6},{5,7},{6,4},{7,5},{8,10},{9,11},{10,... | collective-permute-start | bytes 294920 | tf_op jit(solution)/shard_map/ppermute | solution.py:433
  110.9 16.0 %collective-permute-start.2 = (bf16[8,48,128]{2,1,0:T(8,128)(2,1)S(1)}, bf16[8,48,128]{2,1,0:T(8,128)(2,1)S(1)}, u32[]{:S(2)}, u32[]{:S(2)}) collective-permute-start(bf16[8,48,128]{2,1,0:T(8,128)(2,1)S(1)} %get-tuple-element.19), channel_id=1, source_target_pairs={{0,3},{1,2},{2,1},{3,0},{4,7},{5,6},{6,5},{7,4},{8,11},{9,10},{10,... | collective-permute-start | bytes 294920 | tf_op jit(solution)/shard_map/ppermute | solution.py:433
  113.0 13.9 %collective-permute-start.3 = (bf16[8,48,128]{2,1,0:T(8,128)(2,1)S(1)}, bf16[8,48,128]{2,1,0:T(8,128)(2,1)S(1)}, u32[]{:S(2)}, u32[]{:S(2)}) collective-permute-start(bf16[8,48,128]{2,1,0:T(8,128)(2,1)S(1)} %get-tuple-element.18), channel_id=1, source_target_pairs={{0,4},{1,5},{2,6},{3,7},{4,0},{5,1},{6,2},{7,3},{8,12},{9,13},{10,... | collective-permute-start | bytes 294920 | tf_op jit(solution)/shard_map/ppermute | solution.py:433
  118.0 9.0 %collective-permute-start.4 = (bf16[8,48,128]{2,1,0:T(8,128)(2,1)S(1)}, bf16[8,48,128]{2,1,0:T(8,128)(2,1)S(1)}, u32[]{:S(2)}, u32[]{:S(2)}) collective-permute-start(bf16[8,48,128]{2,1,0:T(8,128)(2,1)S(1)} %get-tuple-element.17), channel_id=1, source_target_pairs={{0,5},{1,4},{2,7},{3,6},{4,1},{5,0},{6,3},{7,2},{8,13},{9,12},{10,... | collective-permute-start | bytes 294920 | tf_op jit(solution)/shard_map/ppermute | solution.py:433
  120.2 9.9 %collective-permute-start.5 = (bf16[8,48,128]{2,1,0:T(8,128)(2,1)S(1)}, bf16[8,48,128]{2,1,0:T(8,128)(2,1)S(1)}, u32[]{:S(2)}, u32[]{:S(2)}) collective-permute-start(bf16[8,48,128]{2,1,0:T(8,128)(2,1)S(1)} %get-tuple-element.16), channel_id=1, source_target_pairs={{0,6},{1,7},{2,4},{3,5},{4,2},{5,3},{6,0},{7,1},{8,14},{9,15},{10,... | collective-permute-start | bytes 294920 | tf_op jit(solution)/shard_map/ppermute | solution.py:433
  125.0 8.6 %collective-permute-start.6 = (bf16[8,48,128]{2,1,0:T(8,128)(2,1)S(1)}, bf16[8,48,128]{2,1,0:T(8,128)(2,1)S(1)}, u32[]{:S(2)}, u32[]{:S(2)}) collective-permute-start(bf16[8,48,128]{2,1,0:T(8,128)(2,1)S(1)} %get-tuple-element.15), channel_id=1, source_target_pairs={{0,7},{1,6},{2,5},{3,4},{4,3},{5,2},{6,1},{7,0},{8,15},{9,14},{10,... | collective-permute-start | bytes 294920 | tf_op jit(solution)/shard_map/ppermute | solution.py:433

commit v4 on v3

--- a/solution.py
+++ b/solution.py
@@ -236,22 +236,16 @@
     for r in range(2):
         for high in range(4):
             for a in range(8):
-                rows = slice(512 * r + 128 * high + 16 * a, 512 * r + 128 * high + 16 * a + 16)
+                rows = slice(128 * high + 16 * a, 128 * high + 16 * a + 16)
                 for t in range(3):
                     first = 768 * high + 6 * a + 2 * t + r
-                    pieces_ref[rows, 128 * t : 128 * t + 128] = wide_ref[
+                    columns = slice(384 * r + 128 * t, 384 * r + 128 * t + 128)
+                    pieces_ref[rows, columns] = wide_ref[
                         pl.ds(first, 16, stride=48), :
                     ].astype(jnp.bfloat16)
     gain = gain_ref[...]
-    parts = []
-    for r in range(2):
-        coeffs = jnp.dot(
-            table_ref[...],
-            pieces_ref[512 * r : 512 * r + 512, :],
-            preferred_element_type=jnp.float32,
-        )
-        parts.append((coeffs * gain).astype(jnp.bfloat16))
-    scaled = jnp.concatenate(parts, axis=1)
+    coeffs = jnp.dot(table_ref[...], pieces_ref[...], preferred_element_type=jnp.float32)
+    scaled = (coeffs * jnp.concatenate([gain, gain], axis=1)).astype(jnp.bfloat16)
     mixed = lax.dot_general(
         weight_ref[...], scaled, (((1,), (1,)), ((), ())), preferred_element_type=jnp.float32
     ).astype(jnp.bfloat16)
@@ -266,7 +260,7 @@
         columns = slice(128 * high, 128 * high + 128)
 
         def group(index, carry, high=high, columns=columns):
-            rows = pl.multiple_of(index * 16, 16)
+            rows = index * 16
             halves = []
             for half in range(2):
                 pieces = []
@@ -284,7 +278,8 @@
                 narrow_ref[here, :] = both.astype(jnp.bfloat16)
             return carry
 
-        lax.fori_loop(0, 3, group, 0)
+        for index in range(3):
+            group(index, 0)
         here = slice(768 * high, 768 * high + 768)
         results.append(
             pltpu.make_async_copy(narrow_ref.at[here], out_ref.at[here], out_sems.at[high])
@@ -304,7 +299,7 @@
         input_output_aliases={4: 0},
         scratch_shapes=[
             pltpu.VMEM((6 * NLAT, 128), jnp.float32),
-            pltpu.VMEM((2 * NLAT, EMBED), jnp.bfloat16),
+            pltpu.VMEM((NLAT, 2 * EMBED), jnp.bfloat16),
             pltpu.VMEM((2 * EMBED, NLAT), jnp.float32),
             pltpu.VMEM((6 * MODES, 128), jnp.bfloat16),
             pltpu.SemaphoreType.DMA((4,)),

time: 153 us -> 152 us (level)
  no operation moved by 1% of the time
where the time goes in v4:
time: 152 us; the launch traced here: 149 us
  waiting for transfers between devices  64.7 us (43%)
  starting transfers between devices  57.9 us (38%)
  Pallas kernels  12.7 us (8%)
  local copies, waits for them, and re-layouts  11.3 us (7%)
    all_to_all x1, waiting for transfers between devices, on_device(): lax.all_to_all(spectrum, both, split_axis=0, concat_axis=0, tiled=True)  35.3 us
    ppermute x7, starting transfers between devices, on_device(): lax.ppermute(grids[k], 'chan', [(i, i ^ k) for i in range(8)])  21.4 us
    all_to_all x1, starting transfers between devices, on_device(): lax.all_to_all(spectrum, both, split_axis=0, concat_axis=0, tiled=True)  21.3 us
    all_to_all x1, waiting for transfers between devices, on_device(): lax.all_to_all(pack_rows(field), both, split_axis=0, concat_axis=0, tiled...  11.9 us
    all_to_all x1, waiting for transfers between devices, on_device(): lax.all_to_all(grid_field, 'chan', split_axis=0, concat_axis=0, tiled=True)  10.9 us
    all_to_all x1, starting transfers between devices, on_device(): lax.all_to_all(pack_rows(field), both, split_axis=0, concat_axis=0, tiled...  10.8 us
    ppermute x7, waiting for transfers between devices, on_device(): lax.ppermute(grids[k], 'chan', [(i, i ^ k) for i in range(8)])  6.63 us
    all_to_all x1, starting transfers between devices, on_device(): lax.all_to_all(grid_field, 'chan', split_axis=0, concat_axis=0, tiled=True)  4.47 us
  transfers between devices with their start and end apart: 10, of which 6 were waited for; matrix products, arithmetic and copies ran while one was open for 7% of the time, Pallas kernels for 3%

profile of v4, /device:TPU:6, one launch (start us, length us, event | category | flops | bytes accessed | tf_op | source)
XLA Modules:
  0.0 148.6 jit_solution(4617186589224703346)
XLA Ops:
  0.0 4.5 %all-to-all-start = ((bf16[8,128,384]{2,1,0:T(8,128)(2,1)}), bf16[8,128,384]{2,1,0:T(8,128)(2,1)S(1)}, u32[]{:S(2)}, u32[]{:S(2)}) async-start(bf16[8,128,384]{2,1,0:T(8,128)(2,1)} %param.10), calls=%async_computation | async-start | bytes 1572864 | tf_op jit(solution)/shard_map/all_to_all | solution.py:413
  4.5 1.6 %copy-done.1 = bf16[1024,1024]{1,0:T(8,128)(2,1)S(1)} copy-done((bf16[1024,1024]{1,0:T(8,128)(2,1)S(1)}, bf16[1024,1024]{1,0:T(8,128)(2,1)}, u32[]{:S(2)}) %copy-start.1) | copy-done | bytes 2097176
  6.7 10.9 %all-to-all-done = bf16[8,128,384]{2,1,0:T(8,128)(2,1)S(1)} async-done(((bf16[8,128,384]{2,1,0:T(8,128)(2,1)}), bf16[8,128,384]{2,1,0:T(8,128)(2,1)S(1)}, u32[]{:S(2)}, u32[]{:S(2)}) %all-to-all-start) | async-done | bytes 786464 | tf_op jit(solution)/shard_map/all_to_all | solution.py:413
  17.7 2.5 %shard_map.101.spare_ref = bf16[3072,128]{1,0:T(8,128)(2,1)} custom-call(f32[4,128]{1,0:T(4,128)S(1)} %copy-done.3, bf16[1024,384]{1,0:T(8,128)(2,1)S(1)} %bitcast.53, f32[1,384]{1,0:T(1,128)S(1)} %reshape.158.gain_ref, bf16[1024,1024]{1,0:T(8,128)(2,1)S(1)} %shard_map.100.table_ref), custom_call_target="tpu_custom_call" | custom-call | flops 800000000 | bytes 4000000 | tf_op jit(solution)/shard_map/pallas_call | solution.py:122
  20.2 21.3 %all-to-all-start.1 = ((bf16[512,2,384]{2,1,0:T(2,128)(2,1)}), bf16[512,2,384]{2,1,0:T(2,128)(2,1)S(1)}, u32[]{:S(2)}, u32[]{:S(2)}) async-start(bf16[512,2,384]{2,1,0:T(2,128)(2,1)} %bitcast.3), calls=%async_computation.1 | async-start | bytes 1572864 | tf_op jit(solution)/shard_map/all_to_all | solution.py:422
  42.8 2.8 %shard_map.102.table_ref = bf16[512,512]{1,0:T(8,128)(2,1)S(1)} custom-call(f32[3,512]{1,0:T(4,128)S(1)} %pad_maximum_fusion.coef_ref, f32[1,512]{1,0:T(1,128)S(1)} %copy-done.2, f32[1,512]{1,0:T(1,128)S(1)} %get-tuple-element.26.start_ref, f32[1,512]{1,0:T(1,128)S(1)} %get-tuple-element.25.exponent_ref), custom_call_target="tpu_custom_call" | custom-call | flops 40000000 | bytes 8000000 | tf_op jit(solution)/shard_map/pallas_call | solution.py:210
  46.2 2.2 %copy.24 = bf16[16,24,2,768]{3,2,1,0:T(2,128)(2,1)} copy(bf16[16,24,2,768]{3,0,1,2:T(8,128)(2,1)S(1)} %bitcast.55) | data formatting | bytes 2359296 | tf_op jit(solution)/shard_map/transpose | solution.py:406
  48.4 3.0 %reshape.164.weight_ref = bf16[768,768]{1,0:T(8,128)(2,1)S(1)} reshape(bf16[16,24,2,768]{3,2,1,0:T(2,128)(2,1)} %copy.24) | data formatting | bytes 2359296 | tf_op jit(solution)/shard_map/reshape | solution.py:406
  51.4 35.3 %all-to-all-done.1 = bf16[512,2,384]{2,1,0:T(2,128)(2,1)S(1)} async-done(((bf16[512,2,384]{2,1,0:T(2,128)(2,1)}), bf16[512,2,384]{2,1,0:T(2,128)(2,1)S(1)}, u32[]{:S(2)}, u32[]{:S(2)}) %all-to-all-start.1) | async-done | bytes 786464 | tf_op jit(solution)/shard_map/all_to_all | solution.py:422
  86.7 3.3 %shard_map.103 = bf16[3072,128]{1,0:T(8,128)(2,1)} custom-call(bf16[3072,128]{1,0:T(8,128)(2,1)S(1)} %bitcast.54, bf16[512,512]{1,0:T(8,128)(2,1)S(1)} %shard_map.102.table_ref, f32[512,384]{1,0:T(8,128)S(1)} %copy-done.4, bf16[768,768]{1,0:T(8,128)(2,1)S(1)} %reshape.164.weight_ref, ...), custom_call_target="tpu_custom_call", output_to_operand_aliasing={{}: (4, {})} | custom-call | flops 1400000000 | bytes 4000000 | tf_op jit(solution)/shard_map/pallas_call | solution.py:294
  90.0 10.8 %all-to-all-start.2 = ((bf16[512,2,384]{2,1,0:T(2,128)(2,1)}), bf16[512,2,384]{2,1,0:T(2,128)(2,1)S(1)}, u32[]{:S(2)}, u32[]{:S(2)}) async-start(bf16[512,2,384]{2,1,0:T(2,128)(2,1)} %bitcast.14), calls=%async_computation.2 | async-start | bytes 1572864 | tf_op jit(solution)/shard_map/all_to_all | solution.py:432
  100.8 2.3 %copy.25 = bf16[8,128,384]{1,2,0:T(8,128)(2,1)} copy(bf16[8,128,384]{2,1,0:T(8,128)(2,1)} %param.10) | data formatting | bytes 1572864 | tf_op jit(solution)/shard_map/optimization_barrier | solution.py:419
  104.4 2.1 %collective-permute-start = (bf16[8,48,128]{2,1,0:T(8,128)(2,1)S(1)}, bf16[8,48,128]{2,1,0:T(8,128)(2,1)S(1)}, u32[]{:S(2)}, u32[]{:S(2)}) collective-permute-start(bf16[8,48,128]{2,1,0:T(8,128)(2,1)S(1)} %get-tuple-element.21), channel_id=1, source_target_pairs={{0,1},{1,0},{2,3},{3,2},{4,5},{5,4},{6,7},{7,6},{8,9},{9,8},{10,11... | collective-permute-start | bytes 294920 | tf_op jit(solution)/shard_map/ppermute | solution.py:428
  106.5 3.5 %collective-permute-start.1 = (bf16[8,48,128]{2,1,0:T(8,128)(2,1)S(1)}, bf16[8,48,128]{2,1,0:T(8,128)(2,1)S(1)}, u32[]{:S(2)}, u32[]{:S(2)}) collective-permute-start(bf16[8,48,128]{2,1,0:T(8,128)(2,1)S(1)} %get-tuple-element.20), channel_id=1, source_target_pairs={{0,2},{1,3},{2,0},{3,1},{4,6},{5,7},{6,4},{7,5},{8,10},{9,11},{10,... | collective-permute-start | bytes 294920 | tf_op jit(solution)/shard_map/ppermute | solution.py:428
  109.9 2.1 %collective-permute-start.2 = (bf16[8,48,128]{2,1,0:T(8,128)(2,1)S(1)}, bf16[8,48,128]{2,1,0:T(8,128)(2,1)S(1)}, u32[]{:S(2)}, u32[]{:S(2)}) collective-permute-start(bf16[8,48,128]{2,1,0:T(8,128)(2,1)S(1)} %get-tuple-element.19), channel_id=1, source_target_pairs={{0,3},{1,2},{2,1},{3,0},{4,7},{5,6},{6,5},{7,4},{8,11},{9,10},{10,... | collective-permute-start | bytes 294920 | tf_op jit(solution)/shard_map/ppermute | solution.py:428
  112.0 5.0 %collective-permute-start.3 = (bf16[8,48,128]{2,1,0:T(8,128)(2,1)S(1)}, bf16[8,48,128]{2,1,0:T(8,128)(2,1)S(1)}, u32[]{:S(2)}, u32[]{:S(2)}) collective-permute-start(bf16[8,48,128]{2,1,0:T(8,128)(2,1)S(1)} %get-tuple-element.18), channel_id=1, source_target_pairs={{0,4},{1,5},{2,6},{3,7},{4,0},{5,1},{6,2},{7,3},{8,12},{9,13},{10,... | collective-permute-start | bytes 294920 | tf_op jit(solution)/shard_map/ppermute | solution.py:428
  117.0 2.1 %collective-permute-start.4 = (bf16[8,48,128]{2,1,0:T(8,128)(2,1)S(1)}, bf16[8,48,128]{2,1,0:T(8,128)(2,1)S(1)}, u32[]{:S(2)}, u32[]{:S(2)}) collective-permute-start(bf16[8,48,128]{2,1,0:T(8,128)(2,1)S(1)} %get-tuple-element.17), channel_id=1, source_target_pairs={{0,5},{1,4},{2,7},{3,6},{4,1},{5,0},{6,3},{7,2},{8,13},{9,12},{10,... | collective-permute-start | bytes 294920 | tf_op jit(solution)/shard_map/ppermute | solution.py:428
  119.2 4.8 %collective-permute-start.5 = (bf16[8,48,128]{2,1,0:T(8,128)(2,1)S(1)}, bf16[8,48,128]{2,1,0:T(8,128)(2,1)S(1)}, u32[]{:S(2)}, u32[]{:S(2)}) collective-permute-start(bf16[8,48,128]{2,1,0:T(8,128)(2,1)S(1)} %get-tuple-element.16), channel_id=1, source_target_pairs={{0,6},{1,7},{2,4},{3,5},{4,2},{5,3},{6,0},{7,1},{8,14},{9,15},{10,... | collective-permute-start | bytes 294920 | tf_op jit(solution)/shard_map/ppermute | solution.py:428
  124.0 1.9 %collective-permute-start.6 = (bf16[8,48,128]{2,1,0:T(8,128)(2,1)S(1)}, bf16[8,48,128]{2,1,0:T(8,128)(2,1)S(1)}, u32[]{:S(2)}, u32[]{:S(2)}) collective-permute-start(bf16[8,48,128]{2,1,0:T(8,128)(2,1)S(1)} %get-tuple-element.15), channel_id=1, source_target_pairs={{0,7},{1,6},{2,5},{3,4},{4,3},{5,2},{6,1},{7,0},{8,15},{9,14},{10,... | collective-permute-start | bytes 294920 | tf_op jit(solution)/shard_map/ppermute | solution.py:428
  126.1 3.0 %collective-permute-done.5.refs_6_ = bf16[8,48,128]{2,1,0:T(8,128)(2,1)S(1)} collective-permute-done((bf16[8,48,128]{2,1,0:T(8,128)(2,1)S(1)}, bf16[8,48,128]{2,1,0:T(8,128)(2,1)S(1)}, u32[]{:S(2)}, u32[]{:S(2)}) %collective-permute-start.5) | collective-permute-done | bytes 98336 | tf_op jit(solution)/shard_map/ppermute | solution.py:428
  129.1 3.5 %collective-permute-done.6.refs_7_ = bf16[8,48,128]{2,1,0:T(8,128)(2,1)S(1)} collective-permute-done((bf16[8,48,128]{2,1,0:T(8,128)(2,1)S(1)}, bf16[8,48,128]{2,1,0:T(8,128)(2,1)S(1)}, u32[]{:S(2)}, u32[]{:S(2)}) %collective-permute-start.6) | collective-permute-done | bytes 98336 | tf_op jit(solution)/shard_map/ppermute | solution.py:428
  132.6 1.6 %shard_map.104.grid_ref = bf16[8,48,1024]{2,1,0:T(8,128)(2,1)} custom-call(s32[8]{0:T(128)S(1)} %iota_xor_fusion.place_ref, bf16[1024,1024]{1,0:T(8,128)(2,1)S(1)} %copy-done, bf16[8,48,128]{2,1,0:T(8,128)(2,1)S(1)} %get-tuple-element.22.refs_0_, bf16[8,48,128]{2,1,0:T(8,128)(2,1)S(1)} %collective-permute-done.refs_1_, ...), custom_call_target="tpu_custom_call" | custom-call | bytes 6000000 | tf_op jit(solution)/shard_map/pallas_call | solution.py:323
  134.2 11.9 %all-to-all-done.2 = bf16[512,2,384]{2,1,0:T(2,128)(2,1)S(1)} async-done(((bf16[512,2,384]{2,1,0:T(2,128)(2,1)}), bf16[512,2,384]{2,1,0:T(2,128)(2,1)S(1)}, u32[]{:S(2)}, u32[]{:S(2)}) %all-to-all-start.2) | async-done | bytes 786464 | tf_op jit(solution)/shard_map/all_to_all | solution.py:432
  146.1 2.3 %shard_map.105 = bf16[8,48,1024]{2,1,0:T(8,128)(2,1)} custom-call(bf16[3072,128]{1,0:T(8,128)(2,1)S(1)} %bitcast.52, bf16[1024,1024]{1,0:T(8,128)(2,1)S(1)} %copy-done, bf16[8,48,1024]{2,1,0:T(8,128)(2,1)} %shard_map.104.grid_ref), custom_call_target="tpu_custom_call", output_to_operand_aliasing={{}: (2, {})} | custom-call | flops 800000000 | bytes 4000000 | tf_op jit(solution)/shard_map/pallas_call | solution.py:382
  (34 shorter events, 4.0 us)
Async XLA Ops:
  0.0 17.6 %all-to-all-start = ((bf16[8,128,384]{2,1,0:T(8,128)(2,1)}), bf16[8,128,384]{2,1,0:T(8,128)(2,1)S(1)}, u32[]{:S(2)}, u32[]{:S(2)}) async-start(bf16[8,128,384]{2,1,0:T(8,128)(2,1)} %param.10), calls=%async_computation | async-start | bytes 1572864 | tf_op jit(solution)/shard_map/all_to_all | solution.py:413
  4.5 1.6 %copy-start.1 = (bf16[1024,1024]{1,0:T(8,128)(2,1)S(1)}, bf16[1024,1024]{1,0:T(8,128)(2,1)}, u32[]{:S(2)}) copy-start(bf16[1024,1024]{1,0:T(8,128)(2,1)} %constant.75.clone.table_ref) | copy-start | bytes 6291460
  6.1 0.7 copy-start.7
  6.1 11.6 %copy-start.3 = (f32[4,128]{1,0:T(4,128)S(1)}, f32[4,128]{1,0:T(4,128)}, u32[]{:S(2)}) copy-start(f32[4,128]{1,0:T(4,128)} %constant.74.clone.weights_ref) | copy-start | bytes 6148
  17.6 23.9 %copy-start.8 = (f32[512]{0:T(512)S(1)}, f32[512]{0:T(512)}, u32[]{:S(2)}) copy-start(f32[512]{0:T(512)} %constant.78.clone) | copy-start | bytes 6148
  17.6 24.5 %copy-start.6 = (f32[1,512]{1,0:T(1,128)S(1)}, f32[1,512]{1,0:T(1,128)}, u32[]{:S(2)}) copy-start(f32[1,512]{1,0:T(1,128)} %constant.77.clone) | copy-start | bytes 6148
  17.6 25.2 %copy-start.2 = (f32[1,512]{1,0:T(1,128)S(1)}, f32[1,512]{1,0:T(1,128)}, u32[]{:S(2)}) copy-start(f32[1,512]{1,0:T(1,128)} %constant.76.clone.cos_ref) | copy-start | bytes 6148
  17.6 28.0 %copy-start.5 = (bf16[2,384,384]{2,1,0:T(8,128)(2,1)S(1)}, bf16[2,384,384]{2,1,0:T(8,128)(2,1)}, u32[]{:S(2)}) copy-start(bf16[2,384,384]{2,1,0:T(8,128)(2,1)} %param.13) | copy-start | bytes 1769476
  20.2 66.5 %all-to-all-start.1 = ((bf16[512,2,384]{2,1,0:T(2,128)(2,1)}), bf16[512,2,384]{2,1,0:T(2,128)(2,1)S(1)}, u32[]{:S(2)}, u32[]{:S(2)}) async-start(bf16[512,2,384]{2,1,0:T(2,128)(2,1)} %bitcast.3), calls=%async_computation.1 | async-start | bytes 1572864 | tf_op jit(solution)/shard_map/all_to_all | solution.py:422
  46.2 40.5 %copy-start.4 = (f32[512,384]{1,0:T(8,128)S(1)}, f32[512,384]{1,0:T(8,128)}, u32[]{:S(2)}) copy-start(f32[512,384]{1,0:T(8,128)} %gain_ref.1) | copy-start | bytes 2359300
  90.0 42.6 %copy-start = (bf16[1024,1024]{1,0:T(8,128)(2,1)S(1)}, bf16[1024,1024]{1,0:T(8,128)(2,1)}, u32[]{:S(2)}) copy-start(bf16[1024,1024]{1,0:T(8,128)(2,1)} %constant.79.clone.table_ref) | copy-start | bytes 6291460
  90.0 56.1 %all-to-all-start.2 = ((bf16[512,2,384]{2,1,0:T(2,128)(2,1)}), bf16[512,2,384]{2,1,0:T(2,128)(2,1)S(1)}, u32[]{:S(2)}, u32[]{:S(2)}) async-start(bf16[512,2,384]{2,1,0:T(2,128)(2,1)} %bitcast.14), calls=%async_computation.2 | async-start | bytes 1572864 | tf_op jit(solution)/shard_map/all_to_all | solution.py:432
  104.4 14.7 %collective-permute-start = (bf16[8,48,128]{2,1,0:T(8,128)(2,1)S(1)}, bf16[8,48,128]{2,1,0:T(8,128)(2,1)S(1)}, u32[]{:S(2)}, u32[]{:S(2)}) collective-permute-start(bf16[8,48,128]{2,1,0:T(8,128)(2,1)S(1)} %get-tuple-element.21), channel_id=1, source_target_pairs={{0,1},{1,0},{2,3},{3,2},{4,5},{5,4},{6,7},{7,6},{8,9},{9,8},{10,11... | collective-permute-start | bytes 294920 | tf_op jit(solution)/shard_map/ppermute | solution.py:428
  106.5 17.5 %collective-permute-start.1 = (bf16[8,48,128]{2,1,0:T(8,128)(2,1)S(1)}, bf16[8,48,128]{2,1,0:T(8,128)(2,1)S(1)}, u32[]{:S(2)}, u32[]{:S(2)}) collective-permute-start(bf16[8,48,128]{2,1,0:T(8,128)(2,1)S(1)} %get-tuple-element.20), channel_id=1, source_target_pairs={{0,2},{1,3},{2,0},{3,1},{4,6},{5,7},{6,4},{7,5},{8,10},{9,11},{10,... | collective-permute-start | bytes 294920 | tf_op jit(solution)/shard_map/ppermute | solution.py:428
  109.9 16.0 %collective-permute-start.2 = (bf16[8,48,128]{2,1,0:T(8,128)(2,1)S(1)}, bf16[8,48,128]{2,1,0:T(8,128)(2,1)S(1)}, u32[]{:S(2)}, u32[]{:S(2)}) collective-permute-start(bf16[8,48,128]{2,1,0:T(8,128)(2,1)S(1)} %get-tuple-element.19), channel_id=1, source_target_pairs={{0,3},{1,2},{2,1},{3,0},{4,7},{5,6},{6,5},{7,4},{8,11},{9,10},{10,... | collective-permute-start | bytes 294920 | tf_op jit(solution)/shard_map/ppermute | solution.py:428
  112.0 13.9 %collective-permute-start.3 = (bf16[8,48,128]{2,1,0:T(8,128)(2,1)S(1)}, bf16[8,48,128]{2,1,0:T(8,128)(2,1)S(1)}, u32[]{:S(2)}, u32[]{:S(2)}) collective-permute-start(bf16[8,48,128]{2,1,0:T(8,128)(2,1)S(1)} %get-tuple-element.18), channel_id=1, source_target_pairs={{0,4},{1,5},{2,6},{3,7},{4,0},{5,1},{6,2},{7,3},{8,12},{9,13},{10,... | collective-permute-start | bytes 294920 | tf_op jit(solution)/shard_map/ppermute | solution.py:428
  117.0 9.0 %collective-permute-start.4 = (bf16[8,48,128]{2,1,0:T(8,128)(2,1)S(1)}, bf16[8,48,128]{2,1,0:T(8,128)(2,1)S(1)}, u32[]{:S(2)}, u32[]{:S(2)}) collective-permute-start(bf16[8,48,128]{2,1,0:T(8,128)(2,1)S(1)} %get-tuple-element.17), channel_id=1, source_target_pairs={{0,5},{1,4},{2,7},{3,6},{4,1},{5,0},{6,3},{7,2},{8,13},{9,12},{10,... | collective-permute-start | bytes 294920 | tf_op jit(solution)/shard_map/ppermute | solution.py:428
  119.2 9.9 %collective-permute-start.5 = (bf16[8,48,128]{2,1,0:T(8,128)(2,1)S(1)}, bf16[8,48,128]{2,1,0:T(8,128)(2,1)S(1)}, u32[]{:S(2)}, u32[]{:S(2)}) collective-permute-start(bf16[8,48,128]{2,1,0:T(8,128)(2,1)S(1)} %get-tuple-element.16), channel_id=1, source_target_pairs={{0,6},{1,7},{2,4},{3,5},{4,2},{5,3},{6,0},{7,1},{8,14},{9,15},{10,... | collective-permute-start | bytes 294920 | tf_op jit(solution)/shard_map/ppermute | solution.py:428
  124.0 8.6 %collective-permute-start.6 = (bf16[8,48,128]{2,1,0:T(8,128)(2,1)S(1)}, bf16[8,48,128]{2,1,0:T(8,128)(2,1)S(1)}, u32[]{:S(2)}, u32[]{:S(2)}) collective-permute-start(bf16[8,48,128]{2,1,0:T(8,128)(2,1)S(1)} %get-tuple-element.15), channel_id=1, source_target_pairs={{0,7},{1,6},{2,5},{3,4},{4,3},{5,2},{6,1},{7,0},{8,15},{9,14},{10,... | collective-permute-start | bytes 294920 | tf_op jit(solution)/shard_map/ppermute | solution.py:428

commit v5 on v4

--- a/solution.py
+++ b/solution.py
@@ -14,6 +14,7 @@
 DEGREES = 512
 MODES = 512
 VMEM_LIMIT = 20 * 1024 * 1024
+WIDE_ROWS = 3072 + 64
 
 
 def grid_points():
@@ -86,21 +87,27 @@
     share = jnp.sum(jnp.where(spot == row, weights_ref[...], 0.0), axis=1, keepdims=True)
     share = jnp.sum(share, axis=0, keepdims=True)
     gain = gain_ref[...]
-    for piece in range(8):
-        rows = slice(128 * piece, 128 * piece + 128)
-        values = grid_ref[rows, :].astype(jnp.float32)
-        mean_value = jnp.mean(values, axis=1, keepdims=True)
-        centered = values - mean_value
-        variance = jnp.mean(centered * centered, axis=1, keepdims=True)
-        normed_ref[rows, :] = (centered * lax.rsqrt(variance + 1e-05) * gain).astype(jnp.bfloat16)
+    sums = [None, None]
+    for part in range(2):
+        for piece in range(4):
+            rows = slice(512 * part + 128 * piece, 512 * part + 128 * piece + 128)
+            values = grid_ref[rows, :].astype(jnp.float32)
+            mean_value = jnp.mean(values, axis=1, keepdims=True)
+            centered = values - mean_value
+            variance = jnp.mean(centered * centered, axis=1, keepdims=True)
+            normed_ref[rows, :] = (centered * lax.rsqrt(variance + 1e-05) * gain).astype(
+                jnp.bfloat16
+            )
+        for half in range(2):
+            term = jnp.dot(
+                table_ref[512 * half : 512 * half + 512, 512 * part : 512 * part + 512],
+                normed_ref[512 * part : 512 * part + 512, :],
+                preferred_element_type=jnp.float32,
+            )
+            sums[half] = term if part == 0 else sums[half] + term
     results = []
     for half in range(2):
-        spectrum = jnp.dot(
-            table_ref[512 * half : 512 * half + 512, :],
-            normed_ref[...],
-            preferred_element_type=jnp.float32,
-        )
-        spectrum = spectrum * share
+        spectrum = sums[half] * share
         first = 1536 * half
         for r in range(2):
             for t in range(3):
@@ -126,7 +133,7 @@
         out_specs=pl.BlockSpec(memory_space=pltpu.MemorySpace.HBM),
         scratch_shapes=[
             pltpu.VMEM((NLON, EMBED), jnp.bfloat16),
-            pltpu.VMEM((6 * MODES, 128), jnp.float32),
+            pltpu.VMEM((WIDE_ROWS, 128), jnp.float32),
             pltpu.VMEM((6 * MODES, 128), jnp.bfloat16),
             pltpu.SemaphoreType.DMA((2,)),
         ],
@@ -138,7 +145,7 @@
 
 
 def spread_rows(source_ref, wide_ref, pieces_ref):
-    wide_ref[...] = source_ref[...].astype(jnp.float32)
+    wide_ref[0:3072, :] = source_ref[...].astype(jnp.float32)
     for r in range(2):
         for t in range(3):
             pieces_ref[512 * r : 512 * r + 512, 128 * t : 128 * t + 128] = wide_ref[
@@ -232,7 +239,7 @@
     narrow_ref,
     out_sems,
 ):
-    wide_ref[...] = arrived_ref[...].astype(jnp.float32)
+    wide_ref[0:3072, :] = arrived_ref[...].astype(jnp.float32)
     for r in range(2):
         for high in range(4):
             for a in range(8):
@@ -298,7 +305,7 @@
         out_specs=pl.BlockSpec(memory_space=pltpu.MemorySpace.HBM),
         input_output_aliases={4: 0},
         scratch_shapes=[
-            pltpu.VMEM((6 * NLAT, 128), jnp.float32),
+            pltpu.VMEM((WIDE_ROWS, 128), jnp.float32),
             pltpu.VMEM((NLAT, 2 * EMBED), jnp.bfloat16),
             pltpu.VMEM((2 * EMBED, NLAT), jnp.float32),
             pltpu.VMEM((6 * MODES, 128), jnp.bfloat16),
@@ -346,12 +353,8 @@
     grid_copy = pltpu.make_async_copy(grid_ref, held_ref, grid_sem)
     grid_copy.start()
     spread_rows(spectrum_ref, wide_ref, pieces_ref)
-    field = lax.dot_general(
-        pieces_ref[...],
-        table_ref[...],
-        (((0,), (0,)), ((), ())),
-        preferred_element_type=jnp.float32,
-    )
+    turned = pieces_ref[...].T
+    field = jnp.dot(turned, table_ref[...], preferred_element_type=jnp.float32)
     for t in range(3):
         for s in range(8):
             columns = slice(128 * s, 128 * s + 128)
@@ -386,7 +389,7 @@
         out_specs=pl.BlockSpec(memory_space=pltpu.MemorySpace.HBM),
         input_output_aliases={2: 0},
         scratch_shapes=[
-            pltpu.VMEM((6 * MODES, 128), jnp.float32),
+            pltpu.VMEM((WIDE_ROWS, 128), jnp.float32),
             pltpu.VMEM((2 * MODES, EMBED), jnp.bfloat16),
             pltpu.VMEM((3 * 144 * 8, 128), jnp.float32),
             pltpu.VMEM((8, 48, NLON), jnp.bfloat16),

time: 152 us -> 152 us (level)
  no operation moved by 1% of the time
where the time goes in v5:
time: 152 us; the launch traced here: 149 us
  waiting for transfers between devices  64.7 us (43%)
  starting transfers between devices  57.9 us (38%)
  Pallas kernels  12.7 us (8%)
  local copies, waits for them, and re-layouts  11.3 us (7%)
    all_to_all x1, waiting for transfers between devices, on_device(): lax.all_to_all(spectrum, both, split_axis=0, concat_axis=0, tiled=True)  35.3 us
    ppermute x7, starting transfers between devices, on_device(): lax.ppermute(grids[k], 'chan', [(i, i ^ k) for i in range(8)])  21.4 us
    all_to_all x1, starting transfers between devices, on_device(): lax.all_to_all(spectrum, both, split_axis=0, concat_axis=0, tiled=True)  21.3 us
    all_to_all x1, waiting for transfers between devices, on_device(): lax.all_to_all(pack_rows(field), both, split_axis=0, concat_axis=0, tiled...  11.9 us
    all_to_all x1, waiting for transfers between devices, on_device(): lax.all_to_all(grid_field, 'chan', split_axis=0, concat_axis=0, tiled=True)  10.9 us
    all_to_all x1, starting transfers between devices, on_device(): lax.all_to_all(pack_rows(field), both, split_axis=0, concat_axis=0, tiled...  10.8 us
    ppermute x7, waiting for transfers between devices, on_device(): lax.ppermute(grids[k], 'chan', [(i, i ^ k) for i in range(8)])  6.63 us
    all_to_all x1, starting transfers between devices, on_device(): lax.all_to_all(grid_field, 'chan', split_axis=0, concat_axis=0, tiled=True)  4.47 us
  transfers between devices with their start and end apart: 10, of which 6 were waited for; matrix products, arithmetic and copies ran while one was open for 7% of the time, Pallas kernels for 3%

profile of v5, /device:TPU:6, one launch (start us, length us, event | category | flops | bytes accessed | tf_op | source)
XLA Modules:
  0.0 148.5 jit_solution(15903905992968758881)
XLA Ops:
  0.0 4.5 %all-to-all-start = ((bf16[8,128,384]{2,1,0:T(8,128)(2,1)}), bf16[8,128,384]{2,1,0:T(8,128)(2,1)S(1)}, u32[]{:S(2)}, u32[]{:S(2)}) async-start(bf16[8,128,384]{2,1,0:T(8,128)(2,1)} %param.10), calls=%async_computation | async-start | bytes 1572864 | tf_op jit(solution)/shard_map/all_to_all | solution.py:416
  4.5 1.6 %copy-done.1 = bf16[1024,1024]{1,0:T(8,128)(2,1)S(1)} copy-done((bf16[1024,1024]{1,0:T(8,128)(2,1)S(1)}, bf16[1024,1024]{1,0:T(8,128)(2,1)}, u32[]{:S(2)}) %copy-start.1) | copy-done | bytes 2097176
  6.7 10.9 %all-to-all-done = bf16[8,128,384]{2,1,0:T(8,128)(2,1)S(1)} async-done(((bf16[8,128,384]{2,1,0:T(8,128)(2,1)}), bf16[8,128,384]{2,1,0:T(8,128)(2,1)S(1)}, u32[]{:S(2)}, u32[]{:S(2)}) %all-to-all-start) | async-done | bytes 786464 | tf_op jit(solution)/shard_map/all_to_all | solution.py:416
  17.7 2.5 %shard_map.101.spare_ref = bf16[3072,128]{1,0:T(8,128)(2,1)} custom-call(f32[4,128]{1,0:T(4,128)S(1)} %copy-done.3, bf16[1024,384]{1,0:T(8,128)(2,1)S(1)} %bitcast.53, f32[1,384]{1,0:T(1,128)S(1)} %reshape.158.gain_ref, bf16[1024,1024]{1,0:T(8,128)(2,1)S(1)} %shard_map.100.table_ref), custom_call_target="tpu_custom_call" | custom-call | flops 800000000 | bytes 4000000 | tf_op jit(solution)/shard_map/pallas_call | solution.py:129
  20.2 21.3 %all-to-all-start.1 = ((bf16[512,2,384]{2,1,0:T(2,128)(2,1)}), bf16[512,2,384]{2,1,0:T(2,128)(2,1)S(1)}, u32[]{:S(2)}, u32[]{:S(2)}) async-start(bf16[512,2,384]{2,1,0:T(2,128)(2,1)} %bitcast.3), calls=%async_computation.1 | async-start | bytes 1572864 | tf_op jit(solution)/shard_map/all_to_all | solution.py:425
  42.8 2.8 %shard_map.102.table_ref = bf16[512,512]{1,0:T(8,128)(2,1)S(1)} custom-call(f32[3,512]{1,0:T(4,128)S(1)} %pad_maximum_fusion.coef_ref, f32[1,512]{1,0:T(1,128)S(1)} %copy-done.2, f32[1,512]{1,0:T(1,128)S(1)} %get-tuple-element.26.start_ref, f32[1,512]{1,0:T(1,128)S(1)} %get-tuple-element.25.exponent_ref), custom_call_target="tpu_custom_call" | custom-call | flops 40000000 | bytes 8000000 | tf_op jit(solution)/shard_map/pallas_call | solution.py:217
  46.2 2.2 %copy.24 = bf16[16,24,2,768]{3,2,1,0:T(2,128)(2,1)} copy(bf16[16,24,2,768]{3,0,1,2:T(8,128)(2,1)S(1)} %bitcast.55) | data formatting | bytes 2359296 | tf_op jit(solution)/shard_map/transpose | solution.py:409
  48.4 3.0 %reshape.164.weight_ref = bf16[768,768]{1,0:T(8,128)(2,1)S(1)} reshape(bf16[16,24,2,768]{3,2,1,0:T(2,128)(2,1)} %copy.24) | data formatting | bytes 2359296 | tf_op jit(solution)/shard_map/reshape | solution.py:409
  51.4 35.3 %all-to-all-done.1 = bf16[512,2,384]{2,1,0:T(2,128)(2,1)S(1)} async-done(((bf16[512,2,384]{2,1,0:T(2,128)(2,1)}), bf16[512,2,384]{2,1,0:T(2,128)(2,1)S(1)}, u32[]{:S(2)}, u32[]{:S(2)}) %all-to-all-start.1) | async-done | bytes 786464 | tf_op jit(solution)/shard_map/all_to_all | solution.py:425
  86.7 3.3 %shard_map.103 = bf16[3072,128]{1,0:T(8,128)(2,1)} custom-call(bf16[3072,128]{1,0:T(8,128)(2,1)S(1)} %bitcast.54, bf16[512,512]{1,0:T(8,128)(2,1)S(1)} %shard_map.102.table_ref, f32[512,384]{1,0:T(8,128)S(1)} %copy-done.4, bf16[768,768]{1,0:T(8,128)(2,1)S(1)} %reshape.164.weight_ref, ...), custom_call_target="tpu_custom_call", output_to_operand_aliasing={{}: (4, {})} | custom-call | flops 1400000000 | bytes 4000000 | tf_op jit(solution)/shard_map/pallas_call | solution.py:301
  90.0 10.8 %all-to-all-start.2 = ((bf16[512,2,384]{2,1,0:T(2,128)(2,1)}), bf16[512,2,384]{2,1,0:T(2,128)(2,1)S(1)}, u32[]{:S(2)}, u32[]{:S(2)}) async-start(bf16[512,2,384]{2,1,0:T(2,128)(2,1)} %bitcast.14), calls=%async_computation.2 | async-start | bytes 1572864 | tf_op jit(solution)/shard_map/all_to_all | solution.py:435
  100.8 2.3 %copy.25 = bf16[8,128,384]{1,2,0:T(8,128)(2,1)} copy(bf16[8,128,384]{2,1,0:T(8,128)(2,1)} %param.10) | data formatting | bytes 1572864 | tf_op jit(solution)/shard_map/optimization_barrier | solution.py:422
  104.4 2.1 %collective-permute-start = (bf16[8,48,128]{2,1,0:T(8,128)(2,1)S(1)}, bf16[8,48,128]{2,1,0:T(8,128)(2,1)S(1)}, u32[]{:S(2)}, u32[]{:S(2)}) collective-permute-start(bf16[8,48,128]{2,1,0:T(8,128)(2,1)S(1)} %get-tuple-element.21), channel_id=1, source_target_pairs={{0,1},{1,0},{2,3},{3,2},{4,5},{5,4},{6,7},{7,6},{8,9},{9,8},{10,11... | collective-permute-start | bytes 294920 | tf_op jit(solution)/shard_map/ppermute | solution.py:431
  106.5 3.5 %collective-permute-start.1 = (bf16[8,48,128]{2,1,0:T(8,128)(2,1)S(1)}, bf16[8,48,128]{2,1,0:T(8,128)(2,1)S(1)}, u32[]{:S(2)}, u32[]{:S(2)}) collective-permute-start(bf16[8,48,128]{2,1,0:T(8,128)(2,1)S(1)} %get-tuple-element.20), channel_id=1, source_target_pairs={{0,2},{1,3},{2,0},{3,1},{4,6},{5,7},{6,4},{7,5},{8,10},{9,11},{10,... | collective-permute-start | bytes 294920 | tf_op jit(solution)/shard_map/ppermute | solution.py:431
  109.9 2.1 %collective-permute-start.2 = (bf16[8,48,128]{2,1,0:T(8,128)(2,1)S(1)}, bf16[8,48,128]{2,1,0:T(8,128)(2,1)S(1)}, u32[]{:S(2)}, u32[]{:S(2)}) collective-permute-start(bf16[8,48,128]{2,1,0:T(8,128)(2,1)S(1)} %get-tuple-element.19), channel_id=1, source_target_pairs={{0,3},{1,2},{2,1},{3,0},{4,7},{5,6},{6,5},{7,4},{8,11},{9,10},{10,... | collective-permute-start | bytes 294920 | tf_op jit(solution)/shard_map/ppermute | solution.py:431
  112.0 5.0 %collective-permute-start.3 = (bf16[8,48,128]{2,1,0:T(8,128)(2,1)S(1)}, bf16[8,48,128]{2,1,0:T(8,128)(2,1)S(1)}, u32[]{:S(2)}, u32[]{:S(2)}) collective-permute-start(bf16[8,48,128]{2,1,0:T(8,128)(2,1)S(1)} %get-tuple-element.18), channel_id=1, source_target_pairs={{0,4},{1,5},{2,6},{3,7},{4,0},{5,1},{6,2},{7,3},{8,12},{9,13},{10,... | collective-permute-start | bytes 294920 | tf_op jit(solution)/shard_map/ppermute | solution.py:431
  117.0 2.1 %collective-permute-start.4 = (bf16[8,48,128]{2,1,0:T(8,128)(2,1)S(1)}, bf16[8,48,128]{2,1,0:T(8,128)(2,1)S(1)}, u32[]{:S(2)}, u32[]{:S(2)}) collective-permute-start(bf16[8,48,128]{2,1,0:T(8,128)(2,1)S(1)} %get-tuple-element.17), channel_id=1, source_target_pairs={{0,5},{1,4},{2,7},{3,6},{4,1},{5,0},{6,3},{7,2},{8,13},{9,12},{10,... | collective-permute-start | bytes 294920 | tf_op jit(solution)/shard_map/ppermute | solution.py:431
  119.1 4.8 %collective-permute-start.5 = (bf16[8,48,128]{2,1,0:T(8,128)(2,1)S(1)}, bf16[8,48,128]{2,1,0:T(8,128)(2,1)S(1)}, u32[]{:S(2)}, u32[]{:S(2)}) collective-permute-start(bf16[8,48,128]{2,1,0:T(8,128)(2,1)S(1)} %get-tuple-element.16), channel_id=1, source_target_pairs={{0,6},{1,7},{2,4},{3,5},{4,2},{5,3},{6,0},{7,1},{8,14},{9,15},{10,... | collective-permute-start | bytes 294920 | tf_op jit(solution)/shard_map/ppermute | solution.py:431
  123.9 1.9 %collective-permute-start.6 = (bf16[8,48,128]{2,1,0:T(8,128)(2,1)S(1)}, bf16[8,48,128]{2,1,0:T(8,128)(2,1)S(1)}, u32[]{:S(2)}, u32[]{:S(2)}) collective-permute-start(bf16[8,48,128]{2,1,0:T(8,128)(2,1)S(1)} %get-tuple-element.15), channel_id=1, source_target_pairs={{0,7},{1,6},{2,5},{3,4},{4,3},{5,2},{6,1},{7,0},{8,15},{9,14},{10,... | collective-permute-start | bytes 294920 | tf_op jit(solution)/shard_map/ppermute | solution.py:431
  126.1 3.0 %collective-permute-done.5.refs_6_ = bf16[8,48,128]{2,1,0:T(8,128)(2,1)S(1)} collective-permute-done((bf16[8,48,128]{2,1,0:T(8,128)(2,1)S(1)}, bf16[8,48,128]{2,1,0:T(8,128)(2,1)S(1)}, u32[]{:S(2)}, u32[]{:S(2)}) %collective-permute-start.5) | collective-permute-done | bytes 98336 | tf_op jit(solution)/shard_map/ppermute | solution.py:431
  129.0 3.5 %collective-permute-done.6.refs_7_ = bf16[8,48,128]{2,1,0:T(8,128)(2,1)S(1)} collective-permute-done((bf16[8,48,128]{2,1,0:T(8,128)(2,1)S(1)}, bf16[8,48,128]{2,1,0:T(8,128)(2,1)S(1)}, u32[]{:S(2)}, u32[]{:S(2)}) %collective-permute-start.6) | collective-permute-done | bytes 98336 | tf_op jit(solution)/shard_map/ppermute | solution.py:431
  132.6 1.6 %shard_map.104.grid_ref = bf16[8,48,1024]{2,1,0:T(8,128)(2,1)} custom-call(s32[8]{0:T(128)S(1)} %iota_xor_fusion.place_ref, bf16[1024,1024]{1,0:T(8,128)(2,1)S(1)} %copy-done, bf16[8,48,128]{2,1,0:T(8,128)(2,1)S(1)} %get-tuple-element.22.refs_0_, bf16[8,48,128]{2,1,0:T(8,128)(2,1)S(1)} %collective-permute-done.refs_1_, ...), custom_call_target="tpu_custom_call" | custom-call | bytes 6000000 | tf_op jit(solution)/shard_map/pallas_call | solution.py:330
  134.2 11.9 %all-to-all-done.2 = bf16[512,2,384]{2,1,0:T(2,128)(2,1)S(1)} async-done(((bf16[512,2,384]{2,1,0:T(2,128)(2,1)}), bf16[512,2,384]{2,1,0:T(2,128)(2,1)S(1)}, u32[]{:S(2)}, u32[]{:S(2)}) %all-to-all-start.2) | async-done | bytes 786464 | tf_op jit(solution)/shard_map/all_to_all | solution.py:435
  146.1 2.3 %shard_map.105 = bf16[8,48,1024]{2,1,0:T(8,128)(2,1)} custom-call(bf16[3072,128]{1,0:T(8,128)(2,1)S(1)} %bitcast.52, bf16[1024,1024]{1,0:T(8,128)(2,1)S(1)} %copy-done, bf16[8,48,1024]{2,1,0:T(8,128)(2,1)} %shard_map.104.grid_ref), custom_call_target="tpu_custom_call", output_to_operand_aliasing={{}: (2, {})} | custom-call | flops 800000000 | bytes 4000000 | tf_op jit(solution)/shard_map/pallas_call | solution.py:385
  (34 shorter events, 4.0 us)
Async XLA Ops:
  0.0 17.6 %all-to-all-start = ((bf16[8,128,384]{2,1,0:T(8,128)(2,1)}), bf16[8,128,384]{2,1,0:T(8,128)(2,1)S(1)}, u32[]{:S(2)}, u32[]{:S(2)}) async-start(bf16[8,128,384]{2,1,0:T(8,128)(2,1)} %param.10), calls=%async_computation | async-start | bytes 1572864 | tf_op jit(solution)/shard_map/all_to_all | solution.py:416
  4.5 1.6 %copy-start.1 = (bf16[1024,1024]{1,0:T(8,128)(2,1)S(1)}, bf16[1024,1024]{1,0:T(8,128)(2,1)}, u32[]{:S(2)}) copy-start(bf16[1024,1024]{1,0:T(8,128)(2,1)} %constant.75.clone.table_ref) | copy-start | bytes 6291460
  6.1 0.7 copy-start.7
  6.1 11.6 %copy-start.3 = (f32[4,128]{1,0:T(4,128)S(1)}, f32[4,128]{1,0:T(4,128)}, u32[]{:S(2)}) copy-start(f32[4,128]{1,0:T(4,128)} %constant.74.clone.weights_ref) | copy-start | bytes 6148
  17.6 23.9 %copy-start.8 = (f32[512]{0:T(512)S(1)}, f32[512]{0:T(512)}, u32[]{:S(2)}) copy-start(f32[512]{0:T(512)} %constant.78.clone) | copy-start | bytes 6148
  17.6 24.5 %copy-start.6 = (f32[1,512]{1,0:T(1,128)S(1)}, f32[1,512]{1,0:T(1,128)}, u32[]{:S(2)}) copy-start(f32[1,512]{1,0:T(1,128)} %constant.77.clone) | copy-start | bytes 6148
  17.6 25.2 %copy-start.2 = (f32[1,512]{1,0:T(1,128)S(1)}, f32[1,512]{1,0:T(1,128)}, u32[]{:S(2)}) copy-start(f32[1,512]{1,0:T(1,128)} %constant.76.clone.cos_ref) | copy-start | bytes 6148
  17.6 28.0 %copy-start.5 = (bf16[2,384,384]{2,1,0:T(8,128)(2,1)S(1)}, bf16[2,384,384]{2,1,0:T(8,128)(2,1)}, u32[]{:S(2)}) copy-start(bf16[2,384,384]{2,1,0:T(8,128)(2,1)} %param.13) | copy-start | bytes 1769476
  20.2 66.5 %all-to-all-start.1 = ((bf16[512,2,384]{2,1,0:T(2,128)(2,1)}), bf16[512,2,384]{2,1,0:T(2,128)(2,1)S(1)}, u32[]{:S(2)}, u32[]{:S(2)}) async-start(bf16[512,2,384]{2,1,0:T(2,128)(2,1)} %bitcast.3), calls=%async_computation.1 | async-start | bytes 1572864 | tf_op jit(solution)/shard_map/all_to_all | solution.py:425
  46.1 40.5 %copy-start.4 = (f32[512,384]{1,0:T(8,128)S(1)}, f32[512,384]{1,0:T(8,128)}, u32[]{:S(2)}) copy-start(f32[512,384]{1,0:T(8,128)} %gain_ref.1) | copy-start | bytes 2359300
  90.0 42.6 %copy-start = (bf16[1024,1024]{1,0:T(8,128)(2,1)S(1)}, bf16[1024,1024]{1,0:T(8,128)(2,1)}, u32[]{:S(2)}) copy-start(bf16[1024,1024]{1,0:T(8,128)(2,1)} %constant.79.clone.table_ref) | copy-start | bytes 6291460
  90.0 56.1 %all-to-all-start.2 = ((bf16[512,2,384]{2,1,0:T(2,128)(2,1)}), bf16[512,2,384]{2,1,0:T(2,128)(2,1)S(1)}, u32[]{:S(2)}, u32[]{:S(2)}) async-start(bf16[512,2,384]{2,1,0:T(2,128)(2,1)} %bitcast.14), calls=%async_computation.2 | async-start | bytes 1572864 | tf_op jit(solution)/shard_map/all_to_all | solution.py:435
  104.4 14.7 %collective-permute-start = (bf16[8,48,128]{2,1,0:T(8,128)(2,1)S(1)}, bf16[8,48,128]{2,1,0:T(8,128)(2,1)S(1)}, u32[]{:S(2)}, u32[]{:S(2)}) collective-permute-start(bf16[8,48,128]{2,1,0:T(8,128)(2,1)S(1)} %get-tuple-element.21), channel_id=1, source_target_pairs={{0,1},{1,0},{2,3},{3,2},{4,5},{5,4},{6,7},{7,6},{8,9},{9,8},{10,11... | collective-permute-start | bytes 294920 | tf_op jit(solution)/shard_map/ppermute | solution.py:431
  106.5 17.5 %collective-permute-start.1 = (bf16[8,48,128]{2,1,0:T(8,128)(2,1)S(1)}, bf16[8,48,128]{2,1,0:T(8,128)(2,1)S(1)}, u32[]{:S(2)}, u32[]{:S(2)}) collective-permute-start(bf16[8,48,128]{2,1,0:T(8,128)(2,1)S(1)} %get-tuple-element.20), channel_id=1, source_target_pairs={{0,2},{1,3},{2,0},{3,1},{4,6},{5,7},{6,4},{7,5},{8,10},{9,11},{10,... | collective-permute-start | bytes 294920 | tf_op jit(solution)/shard_map/ppermute | solution.py:431
  109.9 16.0 %collective-permute-start.2 = (bf16[8,48,128]{2,1,0:T(8,128)(2,1)S(1)}, bf16[8,48,128]{2,1,0:T(8,128)(2,1)S(1)}, u32[]{:S(2)}, u32[]{:S(2)}) collective-permute-start(bf16[8,48,128]{2,1,0:T(8,128)(2,1)S(1)} %get-tuple-element.19), channel_id=1, source_target_pairs={{0,3},{1,2},{2,1},{3,0},{4,7},{5,6},{6,5},{7,4},{8,11},{9,10},{10,... | collective-permute-start | bytes 294920 | tf_op jit(solution)/shard_map/ppermute | solution.py:431
  112.0 13.9 %collective-permute-start.3 = (bf16[8,48,128]{2,1,0:T(8,128)(2,1)S(1)}, bf16[8,48,128]{2,1,0:T(8,128)(2,1)S(1)}, u32[]{:S(2)}, u32[]{:S(2)}) collective-permute-start(bf16[8,48,128]{2,1,0:T(8,128)(2,1)S(1)} %get-tuple-element.18), channel_id=1, source_target_pairs={{0,4},{1,5},{2,6},{3,7},{4,0},{5,1},{6,2},{7,3},{8,12},{9,13},{10,... | collective-permute-start | bytes 294920 | tf_op jit(solution)/shard_map/ppermute | solution.py:431
  117.0 9.0 %collective-permute-start.4 = (bf16[8,48,128]{2,1,0:T(8,128)(2,1)S(1)}, bf16[8,48,128]{2,1,0:T(8,128)(2,1)S(1)}, u32[]{:S(2)}, u32[]{:S(2)}) collective-permute-start(bf16[8,48,128]{2,1,0:T(8,128)(2,1)S(1)} %get-tuple-element.17), channel_id=1, source_target_pairs={{0,5},{1,4},{2,7},{3,6},{4,1},{5,0},{6,3},{7,2},{8,13},{9,12},{10,... | collective-permute-start | bytes 294920 | tf_op jit(solution)/shard_map/ppermute | solution.py:431
  119.1 9.9 %collective-permute-start.5 = (bf16[8,48,128]{2,1,0:T(8,128)(2,1)S(1)}, bf16[8,48,128]{2,1,0:T(8,128)(2,1)S(1)}, u32[]{:S(2)}, u32[]{:S(2)}) collective-permute-start(bf16[8,48,128]{2,1,0:T(8,128)(2,1)S(1)} %get-tuple-element.16), channel_id=1, source_target_pairs={{0,6},{1,7},{2,4},{3,5},{4,2},{5,3},{6,0},{7,1},{8,14},{9,15},{10,... | collective-permute-start | bytes 294920 | tf_op jit(solution)/shard_map/ppermute | solution.py:431
  123.9 8.6 %collective-permute-start.6 = (bf16[8,48,128]{2,1,0:T(8,128)(2,1)S(1)}, bf16[8,48,128]{2,1,0:T(8,128)(2,1)S(1)}, u32[]{:S(2)}, u32[]{:S(2)}) collective-permute-start(bf16[8,48,128]{2,1,0:T(8,128)(2,1)S(1)} %get-tuple-element.15), channel_id=1, source_target_pairs={{0,7},{1,6},{2,5},{3,4},{4,3},{5,2},{6,1},{7,0},{8,15},{9,14},{10,... | collective-permute-start | bytes 294920 | tf_op jit(solution)/shard_map/ppermute | solution.py:431
